TPU v7x, 768 devices: a whole 4x8x12 slice. The times are simulated.
768 devices in a mesh: blk: 96 (over z, y_lo, core), owner: 8 (over y_hi, x).
Axes of the slice: x: 4, y: 8 (y_hi: 2, y_lo: 4; y = y_hi * 4 + y_lo), z: 12, core: 2. Of those that a mesh axis runs over, the one named last changes fastest.
Arguments:
- grad_blocks: bfloat16 [2, 6912, 1024], P(None, 'blk', 'owner'), may hold values from -6 to 6
- ginv_factors: bfloat16 [2, 1024, 1024], P(None, None, 'owner'), as said below
- ainv_owned: bfloat16 [8, 6912, 6912], P('owner', 'blk'), as said below
- owner_table: int32 [2], replicated, may hold values from 0 to 7, as said below
- damp_grad: float32 [2], replicated, may hold values from 0.25 to 2
- damp_act: float32 [2], replicated, may hold values from 0.25 to 2
Outputs:
- preconditioned: bfloat16 [2, 6912, 1024], P(None, 'blk', 'owner')
Inputs may be any that keep to these rules, and one draw needn't show every extreme that they name: `ginv_factors`: each matrix is symmetric and positive definite. `ainv_owned`: each matrix is symmetric and positive definite. `owner_table`: the layers have distinct owners.
All inputs are finite; a program needn't handle non-finite values.
Results may differ from a plain program's by a relative error of at most 0.0049.
Values may be sent and summed in bfloat16 or wider, within the bound.
No kernel may reach another device: no remote copies, remote signals or barrier semaphores. Data moves between devices by JAX's collectives and lax.ppermute only.
A program may use at most 32 MiB of HBM per device.

v0:
```python
import jax
import jax.numpy as jnp
from jax import lax
from jax.sharding import PartitionSpec as P

LAYERS = 2


def broadcast(block, axis, owner):
    block = jnp.where(lax.axis_index(axis) == owner, block, jnp.zeros_like(block))
    return lax.psum(block, axis)


def body(grad_blocks, ginv_factors, ainv_owned, owner_table, damp_grad, damp_act):
    results = []
    for layer_index in range(LAYERS):
        gradient = grad_blocks[layer_index]
        ginv_cols = ginv_factors[layer_index]
        grad_side = jnp.dot(
            lax.all_gather(gradient, "owner", axis=1, tiled=True),
            ginv_cols,
            preferred_element_type=jnp.float32,
        )
        right_side = (grad_side + damp_grad[layer_index] * gradient.astype(jnp.float32)).astype(
            jnp.bfloat16
        )
        factor_rows = broadcast(ainv_owned[0], "owner", owner_table[layer_index])
        act_side = lax.psum_scatter(
            lax.dot_general(
                factor_rows,
                right_side,
                (((0,), (0,)), ((), ())),
                preferred_element_type=jnp.float32,
            ),
            "blk",
            scatter_dimension=0,
            tiled=True,
        )
        finished = act_side + damp_act[layer_index] * right_side.astype(jnp.float32)
        results.append(finished.astype(jnp.bfloat16))
    return jnp.stack(results)


def solution(mesh):
    return jax.shard_map(
        body,
        mesh=mesh,
        in_specs=(
            P(None, "blk", "owner"),
            P(None, None, "owner"),
            P("owner", "blk", None),
            P(),
            P(),
            P(),
        ),
        out_specs=P(None, "blk", "owner"),
        check_vma=False,
    )
```

profile of v0, /device:TPU:1, one launch (start us, length us, event | category | flops | bytes accessed | tf_op | source)
XLA Modules:
  0.0 1010.9 jit_solution(7141397414956981505)
XLA Ops:
  6.5 0.0 copy-start.1
  6.5 0.0 copy-start.2
  6.5 0.0 copy-start.4
  6.5 0.0 all-reduce.5.cloned.1.call-start
  6.5 1.3 fusion.13
  9.2 2.7 select_bitcast_fusion.1
  11.8 0.0 all-reduce.5.cloned.1.call-update
  11.9 0.0 reduce-scatter.9.cloned.1.call-start
  11.9 0.0 copy-done.1
  11.9 41.0 %all-gather = bf16[1,72,1024]{2,1,0:T(8,128)(2,1)S(1)} all-gather(bf16[1,72,128]{2,1,0:T(8,128)(2,1)S(1)} %get-tuple-element.9), channel_id=2, replica_groups=mesh['blk'=96,'owner'=8] {'owner'}, dimensions={2}, use_global_device_ids=true | all-gather | bytes 165888 | tf_op jit(solution)/shard_map/all_gather | solution.py:20
  53.0 0.0 copy-done.2
  53.0 0.6 fusion.12
  53.6 0.0 copy-done.4
  53.6 0.8 fusion
  54.4 103.6 %all-reduce.5.cloned.1.call-done = (bf16[72,6912]{1,0:T(8,128)(2,1)}, bf16[72,6912]{1,0:T(8,128)(2,1)}) async-done(((bf16[72,6912]{1,0:T(8,128)(2,1)}, bf16[72,6912]{1,0:T(8,128)(2,1)}), (bf16[72,6912]{1,0:T(8,128)(2,1)}, bf16[72,6912]{1,0:T(8,128)(2,1)})) %all-reduce.5.cloned.1.call-update) | async-done | bytes 1990672 | tf_op jit(solution)/shard_map/psum | solution.py:11
  158.0 0.0 copy-start
  158.0 3.7 fusion.14
  161.8 0.0 reduce-scatter.9.cloned.1.call-update
  161.8 0.0 reduce-scatter.11.cloned.1.call-start
  161.8 35.0 %all-gather.1 = bf16[1,72,1024]{2,1,0:T(8,128)(2,1)S(1)} all-gather(bf16[1,72,128]{2,1,0:T(8,128)(2,1)S(1)} %get-tuple-element.10), channel_id=3, replica_groups=mesh['blk'=96,'owner'=8] {'owner'}, dimensions={2}, use_global_device_ids=true | all-gather | bytes 165888 | tf_op jit(solution)/shard_map/all_gather | solution.py:20
  196.9 0.8 fusion.1
  197.7 0.0 copy-done
  197.7 0.0 copy-start.3
  197.7 2.5 fusion.15
  200.2 0.0 reduce-scatter.11.cloned.1.call-update
  200.2 0.0 copy-done.3
  200.2 0.6 fusion.11
  200.8 381.4 %reduce-scatter.9.cloned.1.call-done = f32[72,128]{1,0:T(8,128)} async-done(((f32[6912,128]{1,0:T(8,128)}), f32[72,128]{1,0:T(8,128)}) %reduce-scatter.9.cloned.1.call-update) | async-done | bytes 36880
  582.2 1.4 fusion.8
  583.6 418.7 %reduce-scatter.11.cloned.1.call-done = f32[72,128]{1,0:T(8,128)} async-done(((f32[6912,128]{1,0:T(8,128)}), f32[72,128]{1,0:T(8,128)}) %reduce-scatter.11.cloned.1.call-update) | async-done | bytes 36880
  1002.3 1.4 fusion.9
  1003.7 0.6 pad_maximum_fusion
  (1 shorter events, 0.0 us)
Async XLA Ops:
  6.5 5.4 copy-start.1
  6.5 46.4 %copy-start.2 = (f32[2]{0:T(128)S(1)}, f32[2]{0:T(128)}, u32[]{:S(2)}) copy-start(f32[2]{0:T(128)} %param.10) | copy-start | bytes 28
  6.5 47.0 %copy-start.4 = (bf16[2,1024,128]{2,1,0:T(8,128)(2,1)S(1)}, bf16[2,1024,128]{2,1,0:T(8,128)(2,1)}, u32[]{:S(2)}) copy-start(bf16[2,1024,128]{2,1,0:T(8,128)(2,1)} %param.7) | copy-start | bytes 1572868
  6.5 151.5 %all-reduce.5.cloned.1.call-start = ((), (), s32[]{:S(2)}) async-start(), calls=%async_computation.4 | async-start | bytes 3981312 | tf_op jit(solution)/shard_map/psum | solution.py:11
  11.9 570.3 %reduce-scatter.9.cloned.1.call-start = ((), (), s32[]{:S(2)}) async-start(), calls=%async_computation.2 | async-start | bytes 3575808
  158.0 39.6 %copy-start = (bf16[72,6912]{1,0:T(8,128)(2,1)S(1)}, bf16[72,6912]{1,0:T(8,128)(2,1)}, u32[]{:S(2)}) copy-start(bf16[72,6912]{1,0:T(8,128)(2,1)} %get-tuple-element.5) | copy-start | bytes 2985988
  161.8 840.5 %reduce-scatter.11.cloned.1.call-start = ((), (), s32[]{:S(2)}) async-start(), calls=%async_computation.3 | async-start | bytes 3575808
  197.7 2.5 copy-start.3
Sparse Core Ops, SparseCore 0:
  12.0 146.0 all-reduce.4
  161.9 420.2 reduce-scatter.8
  585.3 416.9 reduce-scatter.10
where the time goes:
time: 1020 us; the launch traced here: 1010 us
  waiting for transfers between devices  904 us (89%)
  blocking collectives  76 us (7%)
  between operations  14.4 us (1%)
    unnamed x5, waiting for transfers between devices  800 us
    psum x1, waiting for transfers between devices, broadcast(): return lax.psum(block, axis)  104 us
    all_gather x2, blocking collectives, body(): lax.all_gather(gradient, 'owner', axis=1, tiled=True)  76 us
  transfers between devices with their start and end apart: 3, of which 3 were waited for; matrix products, arithmetic and copies ran while one was open for 1% of the time, Pallas kernels for 0%

commit v1 on v0

v1 whole, which is shorter than its diff:
```python
import numpy as np
import jax
import jax.numpy as jnp
from jax import lax
from jax.sharding import Mesh, PartitionSpec as P

LAYERS = 2
AXES = ("z", "ylo", "core", "yhi", "x")
SIZES = (12, 4, 2, 2, 4)
NZ, NY, NC, NH, NX = SIZES
BLK = ("z", "ylo", "core")
OWNER = ("yhi", "x")
CHUNK = ("ylo", "x")
N_CHUNK = NY * NX
BLOCKS = NZ * NY * NC // N_CHUNK


def flat(z, ylo, core, yhi, x):
    return int(np.ravel_multi_index((z, ylo, core, yhi, x), SIZES))


def spread_pairs():
    pairs = []
    for z, ylo, core, yhi, x in np.ndindex(*SIZES):
        block = (z * NY + ylo) * NC + core
        chunk, part = divmod(block, BLOCKS)
        to_core, to_z = divmod(part * NX + x, NZ)
        to_ylo, to_x = divmod(chunk, NX)
        pairs.append((flat(z, ylo, core, yhi, x), flat(to_z, to_ylo, to_core, yhi, to_x)))
    return pairs


def copies(value, axis, count):
    return lax.all_to_all(jnp.broadcast_to(value[None], (count,) + value.shape), axis, 0, 0)


def body(grad_blocks, ginv_factors, ainv_owned, owner_table, damp_grad, damp_act):
    rows, cols = grad_blocks.shape[1:]
    width = ainv_owned.shape[2] // N_CHUNK
    yhi = lax.axis_index("yhi")
    core = lax.axis_index("core")

    gathered = copies(grad_blocks, OWNER, NH * NX)
    gathered = gathered.transpose(1, 2, 0, 3).reshape(LAYERS, rows, NH * NX * cols)
    right = lax.dot_general(
        gathered, ginv_factors, (((2,), (1,)), ((0,), (0,))), preferred_element_type=jnp.float32
    )
    right = right + damp_grad[:, None, None] * grad_blocks.astype(jnp.float32)
    right = right.astype(jnp.bfloat16)

    factor = ainv_owned[0].reshape(rows, N_CHUNK, width).transpose(1, 0, 2)
    factor = lax.all_to_all(factor, CHUNK, 0, 0).reshape(NY, NX, rows, width)
    owner_half = owner_table // NX
    mine = jnp.stack(
        [
            lax.dynamic_index_in_dim(factor, owner_table[l] % NX, 1, keepdims=False)
            for l in range(LAYERS)
        ]
    ).reshape(LAYERS, NY * rows, width)
    other = lax.ppermute(mine, "yhi", [(0, 1), (1, 0)])
    factor = jnp.where((owner_half == yhi)[:, None, None], mine, other)

    piece = lax.ppermute(right, AXES, spread_pairs())
    along_z = copies(piece, "z", NZ)
    swapped = lax.ppermute(along_z, "core", [(0, 1), (1, 0)])
    first = jnp.where(core == 0, along_z, swapped)
    second = jnp.where(core == 0, swapped, along_z)
    chunk = jnp.stack([first, second]).reshape(BLOCKS, NX, LAYERS, rows, cols)
    chunk = chunk.transpose(2, 0, 3, 1, 4).reshape(LAYERS, BLOCKS * rows, NX * cols)

    partial = lax.dot_general(
        factor, chunk, (((2,), (1,)), ((0,), (0,))), preferred_element_type=jnp.float32
    )
    partial = partial.reshape(LAYERS, NY, rows, NX, cols).transpose(1, 3, 0, 2, 4)
    partial = partial.reshape(N_CHUNK, LAYERS, rows, cols)
    act = jnp.sum(lax.all_to_all(partial, CHUNK, 0, 0), axis=0)
    act = act + damp_act[:, None, None] * right.astype(jnp.float32)
    return act.astype(jnp.bfloat16)


def solution(mesh):
    fine = Mesh(mesh.devices.reshape(SIZES), AXES)
    return jax.shard_map(
        body,
        mesh=fine,
        in_specs=(
            P(None, BLK, OWNER),
            P(None, None, OWNER),
            P(OWNER, BLK, None),
            P(),
            P(),
            P(),
        ),
        out_specs=P(None, BLK, OWNER),
        check_vma=False,
    )
```

time: 1020 us -> 180 us (0.18)
  waiting for transfers between devices: 904 us -> 46.3 us
  starting transfers between devices: 0.09 us -> 39.5 us
  between operations: 14.4 us -> 4.04 us
    unnamed x5 -> x0, waiting for transfers between devices: 800 us -> none
    psum x1 -> x0, waiting for transfers between devices: 104 us -> none  [broadcast(): return lax.psum(block, axis)]
    all_gather x2 -> x0, blocking collectives: 76 us -> none  [body(): lax.all_gather(gradient, 'owner', axis=1, tiled=True)]
    all_to_all x0 -> x2, blocking collectives: none -> 73.8 us  [the longest x1 53.3 us: body(): act = jnp.sum(lax.all_to_all(partial, CHUNK, 0, 0), axis=0)]
    all_to_all x0 -> x2, waiting for transfers between devices: none -> 31 us  [the longest x1 15.6 us: body(): factor = lax.all_to_all(factor, CHUNK, 0, 0).reshape(NY, NX, rows, width)]
    all_to_all x0 -> x2, starting transfers between devices: none -> 20.5 us  [the longest x1 16.8 us: copies(): lax.all_to_all(jnp.broadcast_to(value[None], (count,) + value.shape), axi...]
    ppermute x0 -> x3, starting transfers between devices: none -> 19.1 us  [the longest x1 12.8 us: body(): piece = lax.ppermute(right, AXES, spread_pairs())]
    ppermute x0 -> x3, waiting for transfers between devices: none -> 15.3 us  [the longest x1 14.3 us: body(): other = lax.ppermute(mine, 'yhi', [(0, 1), (1, 0)])]
  transfers between devices with their start and end apart: 3 -> 5, of which waited for: 3 -> 4; matrix products, arithmetic and copies ran while one was open for 1% -> 4% of each run, Pallas kernels for 0% -> 0%
where the time goes in v1:
time: 180 us; the launch traced here: 177 us
  blocking collectives  73.8 us (41%)
  waiting for transfers between devices  46.3 us (26%)
  starting transfers between devices  39.5 us (22%)
  local copies, waits for them, and re-layouts  8.37 us (5%)
  between operations  4.04 us (2%)
  matrix products  2.66 us (1%)
    all_to_all x1, blocking collectives, body(): act = jnp.sum(lax.all_to_all(partial, CHUNK, 0, 0), axis=0)  53.3 us
    all_to_all x1, blocking collectives, copies(): lax.all_to_all(jnp.broadcast_to(value[None], (count,) + value.shape), axi...  20.4 us
    all_to_all x1, starting transfers between devices, copies(): lax.all_to_all(jnp.broadcast_to(value[None], (count,) + value.shape), axi...  16.8 us
    all_to_all x1, waiting for transfers between devices, body(): factor = lax.all_to_all(factor, CHUNK, 0, 0).reshape(NY, NX, rows, width)  15.6 us
    all_to_all x1, waiting for transfers between devices, copies(): lax.all_to_all(jnp.broadcast_to(value[None], (count,) + value.shape), axi...  15.4 us
    ppermute x1, waiting for transfers between devices, body(): other = lax.ppermute(mine, 'yhi', [(0, 1), (1, 0)])  14.3 us
    ppermute x1, starting transfers between devices, body(): piece = lax.ppermute(right, AXES, spread_pairs())  12.8 us
    ppermute x1, starting transfers between devices, body(): swapped = lax.ppermute(along_z, 'core', [(0, 1), (1, 0)])  4.09 us
  transfers between devices with their start and end apart: 5, of which 4 were waited for; matrix products, arithmetic and copies ran while one was open for 4% of the time, Pallas kernels for 0%

profile of v1, /device:TPU:1, one launch (start us, length us, event | category | flops | bytes accessed | tf_op | source)
XLA Modules:
  0.0 176.5 jit_solution(11558128021178945377)
XLA Ops:
  0.0 0.0 copy-start
  0.0 0.9 broadcast_in_dim.13
  0.9 20.4 %all_to_all.20 = bf16[8,2,72,128]{3,2,1,0:T(8,128)(2,1)S(1)} all-to-all(bf16[8,2,72,128]{3,2,1,0:T(8,128)(2,1)S(1)} %broadcast_in_dim.13), channel_id=1, replica_groups=mesh['z'=12,'ylo'=4,'core'=2,'yhi'=2,'x'=4] {'yhi','x'}, dimensions={0} | all-to-all | bytes 589824 | tf_op jit(solution)/shard_map/all_to_all | solution.py:34
  21.3 0.0 copy-done
  21.3 0.0 copy-start.1
  21.3 1.1 fusion
  22.4 12.8 %collective-permute-start.1 = (bf16[2,72,128]{2,1,0:T(8,128)(2,1)S(1)}, bf16[2,72,128]{2,1,0:T(8,128)(2,1)S(1)}, u32[]{:S(2)}, u32[]{:S(2)}) collective-permute-start(bf16[2,72,128]{2,1,0:T(8,128)(2,1)S(1)} %fusion), channel_id=1, source_target_pairs={{0,0},{1,64},{2,128},{3,192},{4,4},{5,68},{6,132},{7,196},{8,256},... | collective-permute-start | bytes 110600 | tf_op jit(solution)/shard_map/ppermute | solution.py:63
  35.2 1.0 collective-permute-done.1
  36.3 0.9 broadcast_in_dim.14
  37.1 16.8 %all-to-all-start.2 = ((bf16[12,2,72,128]{3,2,1,0:T(8,128)(2,1)}), bf16[12,2,72,128]{3,2,1,0:T(8,128)(2,1)S(1)}, u32[]{:S(2)}, u32[]{:S(2)}) async-start(bf16[12,2,72,128]{3,2,1,0:T(8,128)(2,1)} %broadcast_in_dim.14), calls=%async_computation.2 | async-start | bytes 884736 | tf_op jit(solution)/shard_map/all_to_all | solution.py:34
  53.9 0.0 copy-done.1
  53.9 2.6 %reshape_squeeze.3 = bf16[72,16,432]{2,1,0:T(8,128)(2,1)S(1)} reshape(bf16[1,72,6912]{2,1,0:T(8,128)(2,1)S(1)} %copy-done.1) | data formatting | bytes 1990656 | tf_op jit(solution)/shard_map/reshape;squeeze | solution.py:51
  56.5 1.7 copy.16
  58.1 0.0 copy-start.2
  58.1 15.4 %all-to-all-done.2 = bf16[12,2,72,128]{3,2,1,0:T(8,128)(2,1)S(1)} async-done(((bf16[12,2,72,128]{3,2,1,0:T(8,128)(2,1)}), bf16[12,2,72,128]{3,2,1,0:T(8,128)(2,1)S(1)}, u32[]{:S(2)}, u32[]{:S(2)}) %all-to-all-start.2) | async-done | bytes 442400 | tf_op jit(solution)/shard_map/all_to_all | solution.py:34
  73.5 3.7 %all-to-all-start = ((bf16[16,72,432]{2,1,0:T(8,128)(2,1)}), bf16[16,72,432]{2,1,0:T(8,128)(2,1)S(1)}, u32[]{:S(2)}, u32[]{:S(2)}) async-start(bf16[16,72,432]{2,1,0:T(8,128)(2,1)} %copy.16), calls=%async_computation | async-start | bytes 2359296 | tf_op jit(solution)/shard_map/all_to_all | solution.py:52
  77.2 0.0 copy-done.2
  77.2 0.6 fusion.7
  81.7 4.1 %collective-permute-start.2 = (bf16[12,2,72,128]{3,2,1,0:T(8,128)(2,1)S(1)}, bf16[12,2,72,128]{3,2,1,0:T(8,128)(2,1)S(1)}, u32[]{:S(2)}, u32[]{:S(2)}) collective-permute-start(bf16[12,2,72,128]{3,2,1,0:T(8,128)(2,1)S(1)} %all-to-all-done.2), channel_id=1, source_target_pairs={{0,8},{8,0},{1,9},{9,1},{2,10},{10,2},{3,11},{11,3},{4,12},{12,4},... | collective-permute-start | bytes 1327112 | tf_op jit(solution)/shard_map/ppermute | solution.py:65
  85.8 15.6 %all-to-all-done = bf16[16,72,432]{2,1,0:T(8,128)(2,1)S(1)} async-done(((bf16[16,72,432]{2,1,0:T(8,128)(2,1)}), bf16[16,72,432]{2,1,0:T(8,128)(2,1)S(1)}, u32[]{:S(2)}, u32[]{:S(2)}) %all-to-all-start) | async-done | bytes 995360 | tf_op jit(solution)/shard_map/all_to_all | solution.py:52
  101.5 0.9 pad_maximum_fusion.1
  102.4 2.2 %collective-permute-start = (bf16[2,288,432]{2,1,0:T(8,128)(2,1)}, bf16[2,288,432]{2,1,0:T(8,128)(2,1)}, u32[]{:S(2)}, u32[]{:S(2)}) collective-permute-start(bf16[2,288,432]{2,1,0:T(8,128)(2,1)} %pad_maximum_fusion.1), channel_id=1, source_target_pairs={{0,4},{4,0},{1,5},{5,1},{2,6},{6,2},{3,7},{7,3},{8,12},{12,8},{9,1... | collective-permute-start | bytes 1493000 | tf_op jit(solution)/shard_map/ppermute | solution.py:60
  104.6 0.0 collective-permute-done.2
  104.6 0.1 select_bitcast_fusion.1
  104.7 0.1 pad_maximum_fusion
  104.8 0.3 copy.18
  105.1 0.3 reshape.33
  105.5 14.3 %collective-permute-done = bf16[2,288,432]{2,1,0:T(8,128)(2,1)} collective-permute-done((bf16[2,288,432]{2,1,0:T(8,128)(2,1)}, bf16[2,288,432]{2,1,0:T(8,128)(2,1)}, u32[]{:S(2)}, u32[]{:S(2)}) %collective-permute-start) | collective-permute-done | bytes 497696 | tf_op jit(solution)/shard_map/ppermute | solution.py:60
  119.7 1.6 fusion.1
  121.3 0.4 reshape.34
  121.7 0.1 copy.19
  121.8 53.3 %all_to_all.21 = f32[16,2,72,128]{3,2,1,0:T(8,128)S(1)} all-to-all(f32[16,2,72,128]{3,2,1,0:T(8,128)S(1)} %bitcast.26), channel_id=1, replica_groups=mesh['z'=12,'ylo'=4,'core'=2,'yhi'=2,'x'=4] {'ylo','x'}, dimensions={0} | all-to-all | bytes 2359296 | tf_op jit(solution)/shard_map/all_to_all | solution.py:76
  175.2 0.0 copy-start.3
  175.2 0.1 reduce_sum.9
  175.2 0.6 copy-done.3
  175.8 0.7 add_convert_fusion
  (2 shorter events, 0.1 us)
Async XLA Ops:
  0.0 21.3 %copy-start = (bf16[2,1024,128]{2,1,0:T(8,128)(2,1)S(1)}, bf16[2,1024,128]{2,1,0:T(8,128)(2,1)}, u32[]{:S(2)}) copy-start(bf16[2,1024,128]{2,1,0:T(8,128)(2,1)} %param.7) | copy-start | bytes 1572868
  21.3 32.6 %copy-start.1 = (bf16[1,72,6912]{2,1,0:T(8,128)(2,1)S(1)}, bf16[1,72,6912]{2,1,0:T(8,128)(2,1)}, u32[]{:S(2)}) copy-start(bf16[1,72,6912]{2,1,0:T(8,128)(2,1)} %param.8) | copy-start | bytes 2985988
  22.4 13.8 %collective-permute-start.1 = (bf16[2,72,128]{2,1,0:T(8,128)(2,1)S(1)}, bf16[2,72,128]{2,1,0:T(8,128)(2,1)S(1)}, u32[]{:S(2)}, u32[]{:S(2)}) collective-permute-start(bf16[2,72,128]{2,1,0:T(8,128)(2,1)S(1)} %fusion), channel_id=1, source_target_pairs={{0,0},{1,64},{2,128},{3,192},{4,4},{5,68},{6,132},{7,196},{8,256},... | collective-permute-start | bytes 110600 | tf_op jit(solution)/shard_map/ppermute | solution.py:63
  37.1 36.4 %all-to-all-start.2 = ((bf16[12,2,72,128]{3,2,1,0:T(8,128)(2,1)}), bf16[12,2,72,128]{3,2,1,0:T(8,128)(2,1)S(1)}, u32[]{:S(2)}, u32[]{:S(2)}) async-start(bf16[12,2,72,128]{3,2,1,0:T(8,128)(2,1)} %broadcast_in_dim.14), calls=%async_computation.2 | async-start | bytes 884736 | tf_op jit(solution)/shard_map/all_to_all | solution.py:34
  58.1 19.1 %copy-start.2 = (s32[2]{0:T(128)S(1)}, s32[2]{0:T(128)}, u32[]{:S(2)}) copy-start(s32[2]{0:T(128)} %param.9) | copy-start | bytes 28
  73.5 27.9 %all-to-all-start = ((bf16[16,72,432]{2,1,0:T(8,128)(2,1)}), bf16[16,72,432]{2,1,0:T(8,128)(2,1)S(1)}, u32[]{:S(2)}, u32[]{:S(2)}) async-start(bf16[16,72,432]{2,1,0:T(8,128)(2,1)} %copy.16), calls=%async_computation | async-start | bytes 2359296 | tf_op jit(solution)/shard_map/all_to_all | solution.py:52
  81.7 22.9 %collective-permute-start.2 = (bf16[12,2,72,128]{3,2,1,0:T(8,128)(2,1)S(1)}, bf16[12,2,72,128]{3,2,1,0:T(8,128)(2,1)S(1)}, u32[]{:S(2)}, u32[]{:S(2)}) collective-permute-start(bf16[12,2,72,128]{3,2,1,0:T(8,128)(2,1)S(1)} %all-to-all-done.2), channel_id=1, source_target_pairs={{0,8},{8,0},{1,9},{9,1},{2,10},{10,2},{3,11},{11,3},{4,12},{12,4},... | collective-permute-start | bytes 1327112 | tf_op jit(solution)/shard_map/ppermute | solution.py:65
  102.4 17.4 %collective-permute-start = (bf16[2,288,432]{2,1,0:T(8,128)(2,1)}, bf16[2,288,432]{2,1,0:T(8,128)(2,1)}, u32[]{:S(2)}, u32[]{:S(2)}) collective-permute-start(bf16[2,288,432]{2,1,0:T(8,128)(2,1)} %pad_maximum_fusion.1), channel_id=1, source_target_pairs={{0,4},{4,0},{1,5},{5,1},{2,6},{6,2},{3,7},{7,3},{8,12},{12,8},{9,1... | collective-permute-start | bytes 1493000 | tf_op jit(solution)/shard_map/ppermute | solution.py:60
  175.2 0.7 copy-start.3

commit v2 on v1

v2 whole, which is shorter than its diff:
```python
import numpy as np
import jax
import jax.numpy as jnp
from jax import lax
from jax.sharding import Mesh, PartitionSpec as P

LAYERS = 2
AXES = ("za", "zb", "ya", "yb", "core", "yhi", "x")
SIZES = (6, 2, 2, 2, 2, 2, 4)
NX = 4
N_OWNER = 8
BLK = ("za", "zb", "ya", "yb", "core")
OWNER = ("yhi", "x")
CHUNK = ("zb", "yb", "x")
MEMBERS = ("za", "ya")
N_CHUNK = 16
N_ROWS = 4
BLOCKS = 6
N_MEMBER = 12


def flat(*index):
    return int(np.ravel_multi_index(index, SIZES))


def spread_pairs():
    pairs = []
    for index in np.ndindex(*SIZES):
        block = int(np.ravel_multi_index(index[:5], SIZES[:5]))
        yhi, x = index[5:]
        chunk, part = divmod(block, BLOCKS)
        to_core, member = divmod(part * NX + x, N_MEMBER)
        to_za, to_ya = divmod(member, 2)
        to_zb, to_yb, to_x = np.unravel_index(chunk, (2, 2, NX))
        pairs.append((flat(*index), flat(to_za, to_zb, to_ya, to_yb, to_core, yhi, to_x)))
    return pairs


def copies(value, axis, count):
    return lax.all_to_all(jnp.broadcast_to(value[None], (count,) + value.shape), axis, 0, 0)


def body(grad_blocks, ginv_factors, ainv_owned, owner_table, damp_grad, damp_act):
    rows, cols = grad_blocks.shape[1:]
    width = ainv_owned.shape[2] // N_CHUNK
    yhi = lax.axis_index("yhi")
    core = lax.axis_index("core")

    factor = ainv_owned[0].reshape(rows, N_CHUNK, width).transpose(1, 0, 2)
    factor = lax.all_to_all(factor, CHUNK, 0, 0).reshape(N_ROWS, NX, rows, width)
    owner_half = owner_table // NX
    mine = jnp.stack(
        [
            lax.dynamic_index_in_dim(factor, owner_table[l] % NX, 1, keepdims=False)
            for l in range(LAYERS)
        ]
    ).reshape(LAYERS, N_ROWS * rows, width)
    mine, gradient = lax.optimization_barrier((mine, grad_blocks))
    other = lax.ppermute(mine, "yhi", [(0, 1), (1, 0)])

    gathered = copies(gradient, OWNER, N_OWNER)
    gathered = gathered.transpose(1, 2, 0, 3).reshape(LAYERS, rows, N_OWNER * cols)
    right = lax.dot_general(
        gathered, ginv_factors, (((2,), (1,)), ((0,), (0,))), preferred_element_type=jnp.float32
    )
    right = right + damp_grad[:, None, None] * grad_blocks.astype(jnp.float32)
    right = right.astype(jnp.bfloat16)
    piece = lax.ppermute(right, AXES, spread_pairs())
    other, piece = lax.optimization_barrier((other, piece))
    factor = jnp.where((owner_half == yhi)[:, None, None], mine, other)

    along_z = copies(piece, MEMBERS, N_MEMBER)
    swapped = lax.ppermute(along_z, "core", [(0, 1), (1, 0)])
    first = jnp.where(core == 0, along_z, swapped)
    second = jnp.where(core == 0, swapped, along_z)
    chunk = jnp.stack([first, second]).reshape(BLOCKS, NX, LAYERS, rows, cols)
    chunk = chunk.transpose(2, 0, 3, 1, 4).reshape(LAYERS, BLOCKS * rows, NX * cols)

    partial = lax.dot_general(
        factor, chunk, (((2,), (1,)), ((0,), (0,))), preferred_element_type=jnp.float32
    )
    partial = partial.reshape(LAYERS, N_ROWS, rows, NX, cols).transpose(1, 3, 0, 2, 4)
    partial = partial.reshape(N_CHUNK, LAYERS, rows, cols)
    act = jnp.sum(lax.all_to_all(partial, CHUNK, 0, 0), axis=0)
    act = act + damp_act[:, None, None] * right.astype(jnp.float32)
    return act.astype(jnp.bfloat16)


def solution(mesh):
    fine = Mesh(mesh.devices.reshape(SIZES), AXES)
    return jax.shard_map(
        body,
        mesh=fine,
        in_specs=(
            P(None, BLK, OWNER),
            P(None, None, OWNER),
            P(OWNER, BLK, None),
            P(),
            P(),
            P(),
        ),
        out_specs=P(None, BLK, OWNER),
        check_vma=False,
    )
```

time: 180 us -> 148 us (0.82); the launches traced: 177 us -> 147 us
  waiting for transfers between devices: 46.3 us -> 22.1 us
  blocking collectives: 73.8 us -> 56.9 us
  starting transfers between devices: 39.5 us -> 51.6 us
    all_to_all x1, blocking collectives: 53.3 us -> 27.7 us  [body(): act = jnp.sum(lax.all_to_all(partial, CHUNK, 0, 0), axis=0)]
    all_to_all x1, waiting for transfers between devices: 15.4 us -> 2.87 us  [copies(): lax.all_to_all(jnp.broadcast_to(value[None], (count,) + value.shape), axi...]
    all_to_all x1, blocking collectives: 20.4 us -> 29.2 us  [copies(): lax.all_to_all(jnp.broadcast_to(value[None], (count,) + value.shape), axi...]
    all_to_all x1, waiting for transfers between devices: 15.6 us -> 8.58 us  [body(): lax.all_to_all(factor, CHUNK, 0, 0).reshape(N_ROWS, NX, rows, width)]
    all_to_all x1, starting transfers between devices: 16.8 us -> 10.5 us  [copies(): lax.all_to_all(jnp.broadcast_to(value[None], (count,) + value.shape), axi...]
    ppermute x1, starting transfers between devices: 4.09 us -> 9.66 us  [body(): swapped = lax.ppermute(along_z, 'core', [(0, 1), (1, 0)])]
    ppermute x1, starting transfers between devices: 2.21 us -> 7.27 us  [body(): other = lax.ppermute(mine, 'yhi', [(0, 1), (1, 0)])]
    ppermute x1, waiting for transfers between devices: 14.3 us -> 9.24 us  [body(): other = lax.ppermute(mine, 'yhi', [(0, 1), (1, 0)])]
  transfers between devices with their start and end apart: 5 -> 5, of which waited for: 4 -> 4; matrix products, arithmetic and copies ran while one was open for 4% -> 1% of each run, Pallas kernels for 0% -> 0%
where the time goes in v2:
time: 148 us; the launch traced here: 147 us
  blocking collectives  56.9 us (38%)
  starting transfers between devices  51.6 us (35%)
  waiting for transfers between devices  22.1 us (15%)
  local copies, waits for them, and re-layouts  10.1 us (7%)
  between operations  3.77 us (3%)
  matrix products  1.8 us (1%)
    all_to_all x1, blocking collectives, copies(): lax.all_to_all(jnp.broadcast_to(value[None], (count,) + value.shape), axi...  29.2 us
    all_to_all x1, blocking collectives, body(): act = jnp.sum(lax.all_to_all(partial, CHUNK, 0, 0), axis=0)  27.7 us
    ppermute x1, starting transfers between devices, body(): piece = lax.ppermute(right, AXES, spread_pairs())  16.2 us
    all_to_all x1, starting transfers between devices, copies(): lax.all_to_all(jnp.broadcast_to(value[None], (count,) + value.shape), axi...  10.5 us
    ppermute x1, starting transfers between devices, body(): swapped = lax.ppermute(along_z, 'core', [(0, 1), (1, 0)])  9.66 us
    ppermute x1, waiting for transfers between devices, body(): other = lax.ppermute(mine, 'yhi', [(0, 1), (1, 0)])  9.24 us
    all_to_all x1, waiting for transfers between devices, body(): lax.all_to_all(factor, CHUNK, 0, 0).reshape(N_ROWS, NX, rows, width)  8.58 us
    all_to_all x1, starting transfers between devices, body(): lax.all_to_all(factor, CHUNK, 0, 0).reshape(N_ROWS, NX, rows, width)  7.91 us
  transfers between devices with their start and end apart: 5, of which 4 were waited for; matrix products, arithmetic and copies ran while one was open for 1% of the time, Pallas kernels for 0%

profile of v2, /device:TPU:1, one launch (start us, length us, event | category | flops | bytes accessed | tf_op | source)
XLA Modules:
  0.0 147.2 jit_solution(10000938989756834158)
XLA Ops:
  0.0 0.0 copy-start
  0.0 3.8 %reshape_squeeze.3 = bf16[72,16,432]{2,1,0:T(8,128)(2,1)S(1)} reshape(bf16[1,72,6912]{2,1,0:T(8,128)(2,1)} %param.8) | data formatting | bytes 1990656 | tf_op jit(solution)/shard_map/reshape;squeeze | solution.py:49
  3.8 1.7 %copy.16 = bf16[16,72,432]{2,1,0:T(8,128)(2,1)} copy(bf16[16,72,432]{2,0,1:T(8,128)(2,1)S(1)} %bitcast.27) | data formatting | bytes 1990656 | tf_op jit(solution)/shard_map/transpose | solution.py:49
  5.5 0.0 copy-start.3
  5.5 7.9 %all-to-all-start = ((bf16[16,72,432]{2,1,0:T(8,128)(2,1)}), bf16[16,72,432]{2,1,0:T(8,128)(2,1)S(1)}, u32[]{:S(2)}, u32[]{:S(2)}) async-start(bf16[16,72,432]{2,1,0:T(8,128)(2,1)} %copy.16), calls=%async_computation | async-start | bytes 2359296 | tf_op jit(solution)/shard_map/all_to_all | solution.py:50
  13.4 0.0 copy-done.3
  13.4 0.6 fusion.7
  17.6 8.6 %all-to-all-done = bf16[16,72,432]{2,1,0:T(8,128)(2,1)S(1)} async-done(((bf16[16,72,432]{2,1,0:T(8,128)(2,1)}), bf16[16,72,432]{2,1,0:T(8,128)(2,1)S(1)}, u32[]{:S(2)}, u32[]{:S(2)}) %all-to-all-start) | async-done | bytes 995360 | tf_op jit(solution)/shard_map/all_to_all | solution.py:50
  26.2 0.0 copy-start.2
  26.2 0.0 copy-start.4
  26.2 0.1 pad_maximum_fusion.1
  26.3 0.6 copy-done.2
  26.9 0.8 broadcast_in_dim.13
  27.7 10.5 %all-to-all-start.1 = ((bf16[8,2,72,128]{3,2,1,0:T(8,128)(2,1)}), bf16[8,2,72,128]{3,2,1,0:T(8,128)(2,1)S(1)}, u32[]{:S(2)}, u32[]{:S(2)}) async-start(bf16[8,2,72,128]{3,2,1,0:T(8,128)(2,1)} %broadcast_in_dim.13), calls=%async_computation.1 | async-start | bytes 589824 | tf_op jit(solution)/shard_map/all_to_all | solution.py:40
  38.2 7.3 %collective-permute-start = (bf16[2,288,432]{2,1,0:T(8,128)(2,1)S(1)}, bf16[2,288,432]{2,1,0:T(8,128)(2,1)S(1)}, u32[]{:S(2)}, u32[]{:S(2)}) collective-permute-start(bf16[2,288,432]{2,1,0:T(8,128)(2,1)S(1)} %pad_maximum_fusion.1), channel_id=1, source_target_pairs={{0,4},{4,0},{1,5},{5,1},{2,6},{6,2},{3,7},{7,3},{8,12},{12,8},{9,1... | collective-permute-start | bytes 1493000 | tf_op jit(solution)/shard_map/ppermute | solution.py:59
  45.5 2.9 %all-to-all-done.1 = bf16[8,2,72,128]{3,2,1,0:T(8,128)(2,1)S(1)} async-done(((bf16[8,2,72,128]{3,2,1,0:T(8,128)(2,1)}), bf16[8,2,72,128]{3,2,1,0:T(8,128)(2,1)S(1)}, u32[]{:S(2)}, u32[]{:S(2)}) %all-to-all-start.1) | async-done | bytes 294944 | tf_op jit(solution)/shard_map/all_to_all | solution.py:40
  48.4 0.0 copy-done
  48.4 0.0 copy-done.4
  48.4 0.2 fusion
  48.6 16.2 %collective-permute-start.1 = (bf16[2,72,128]{2,1,0:T(8,128)(2,1)S(1)}, bf16[2,72,128]{2,1,0:T(8,128)(2,1)S(1)}, u32[]{:S(2)}, u32[]{:S(2)}) collective-permute-start(bf16[2,72,128]{2,1,0:T(8,128)(2,1)S(1)} %fusion), channel_id=1, source_target_pairs={{0,0},{1,32},{2,128},{3,160},{4,4},{5,36},{6,132},{7,164},{8,256},... | collective-permute-start | bytes 110600 | tf_op jit(solution)/shard_map/ppermute | solution.py:68
  64.8 9.2 %collective-permute-done = bf16[2,288,432]{2,1,0:T(8,128)(2,1)S(1)} collective-permute-done((bf16[2,288,432]{2,1,0:T(8,128)(2,1)S(1)}, bf16[2,288,432]{2,1,0:T(8,128)(2,1)S(1)}, u32[]{:S(2)}, u32[]{:S(2)}) %collective-permute-start) | collective-permute-done | bytes 497696 | tf_op jit(solution)/shard_map/ppermute | solution.py:59
  74.0 0.0 copy-start.1
  74.0 0.0 collective-permute-done.1
  74.0 0.8 copy-done.1
  74.9 0.1 broadcast_in_dim.14
  74.9 29.2 %all_to_all.20 = bf16[12,2,72,128]{3,2,1,0:T(8,128)(2,1)S(1)} all-to-all(bf16[12,2,72,128]{3,2,1,0:T(8,128)(2,1)S(1)} %broadcast_in_dim.14), channel_id=1, replica_groups=mesh['za'=6,'zb'=2,'ya'=2,'yb'=2,'core'=2,'yhi'=2,'x'=4] {'za','ya'}, dimensions={0} | all-to-all | bytes 884736 | tf_op jit(solution)/shard_map/all_to_all | solution.py:40
  104.1 9.7 %collective-permute-start.2 = (bf16[12,2,72,128]{3,2,1,0:T(8,128)(2,1)S(1)}, bf16[12,2,72,128]{3,2,1,0:T(8,128)(2,1)S(1)}, u32[]{:S(2)}, u32[]{:S(2)}) collective-permute-start(bf16[12,2,72,128]{3,2,1,0:T(8,128)(2,1)S(1)} %all_to_all.20), channel_id=1, source_target_pairs={{0,8},{8,0},{1,9},{9,1},{2,10},{10,2},{3,11},{11,3},{4,12},{12,4},... | collective-permute-start | bytes 1327112 | tf_op jit(solution)/shard_map/ppermute | solution.py:73
  113.8 1.4 collective-permute-done.2
  115.2 0.1 select_bitcast_fusion.1
  115.2 0.1 pad_maximum_fusion
  115.3 0.3 copy.18
  115.7 0.3 reshape.33
  116.0 1.6 %fusion.1 = f32[2,288,512]{2,1,0:T(8,128)S(1)} fusion(bf16[2,432,512]{2,1,0:T(8,128)(2,1)S(1)} %reshape.33, bf16[2,288,432]{2,1,0:T(8,128)(2,1)S(1)} %pad_maximum_fusion.1, bf16[2,288,432]{2,1,0:T(8,128)(2,1)} %copy-done.1, pred[2]{0:T(512)(128)(4,1)S(1)} %fusion.6), kind=kOutput, calls=%fused_computation.4 | convolution fusion | flops 255052800 | bytes 3059714 | tf_op jit(solution)/shard_map/dot_general | solution.py:79
  117.6 0.4 reshape.34
  118.0 0.1 copy.19
  118.1 27.7 %all_to_all.21 = f32[16,2,72,128]{3,2,1,0:T(8,128)S(1)} all-to-all(f32[16,2,72,128]{3,2,1,0:T(8,128)S(1)} %bitcast.26), channel_id=1, replica_groups=mesh['za'=6,'zb'=2,'ya'=2,'yb'=2,'core'=2,'yhi'=2,'x'=4] {'zb','yb','x'}, dimensions={0} | all-to-all | bytes 2359296 | tf_op jit(solution)/shard_map/all_to_all | solution.py:84
  145.8 0.0 copy-start.5
  145.8 0.1 reduce_sum.9
  145.9 0.6 copy-done.5
  146.5 0.7 add_convert_fusion
  (2 shorter events, 0.1 us)
Async XLA Ops:
  0.0 48.4 %copy-start = (bf16[2,1024,128]{2,1,0:T(8,128)(2,1)S(1)}, bf16[2,1024,128]{2,1,0:T(8,128)(2,1)}, u32[]{:S(2)}) copy-start(bf16[2,1024,128]{2,1,0:T(8,128)(2,1)} %param.7) | copy-start | bytes 1572868
  5.5 7.9 %copy-start.3 = (s32[2]{0:T(128)S(1)}, s32[2]{0:T(128)}, u32[]{:S(2)}) copy-start(s32[2]{0:T(128)} %param.9) | copy-start | bytes 28
  5.5 20.7 %all-to-all-start = ((bf16[16,72,432]{2,1,0:T(8,128)(2,1)}), bf16[16,72,432]{2,1,0:T(8,128)(2,1)S(1)}, u32[]{:S(2)}, u32[]{:S(2)}) async-start(bf16[16,72,432]{2,1,0:T(8,128)(2,1)} %copy.16), calls=%async_computation | async-start | bytes 2359296 | tf_op jit(solution)/shard_map/all_to_all | solution.py:50
  26.2 0.8 copy-start.2
  26.2 22.1 %copy-start.4 = (f32[2]{0:T(128)S(1)}, f32[2]{0:T(128)}, u32[]{:S(2)}) copy-start(f32[2]{0:T(128)} %param.10) | copy-start | bytes 28
  27.7 20.7 %all-to-all-start.1 = ((bf16[8,2,72,128]{3,2,1,0:T(8,128)(2,1)}), bf16[8,2,72,128]{3,2,1,0:T(8,128)(2,1)S(1)}, u32[]{:S(2)}, u32[]{:S(2)}) async-start(bf16[8,2,72,128]{3,2,1,0:T(8,128)(2,1)} %broadcast_in_dim.13), calls=%async_computation.1 | async-start | bytes 589824 | tf_op jit(solution)/shard_map/all_to_all | solution.py:40
  38.2 35.8 %collective-permute-start = (bf16[2,288,432]{2,1,0:T(8,128)(2,1)S(1)}, bf16[2,288,432]{2,1,0:T(8,128)(2,1)S(1)}, u32[]{:S(2)}, u32[]{:S(2)}) collective-permute-start(bf16[2,288,432]{2,1,0:T(8,128)(2,1)S(1)} %pad_maximum_fusion.1), channel_id=1, source_target_pairs={{0,4},{4,0},{1,5},{5,1},{2,6},{6,2},{3,7},{7,3},{8,12},{12,8},{9,1... | collective-permute-start | bytes 1493000 | tf_op jit(solution)/shard_map/ppermute | solution.py:59
  48.6 25.4 %collective-permute-start.1 = (bf16[2,72,128]{2,1,0:T(8,128)(2,1)S(1)}, bf16[2,72,128]{2,1,0:T(8,128)(2,1)S(1)}, u32[]{:S(2)}, u32[]{:S(2)}) collective-permute-start(bf16[2,72,128]{2,1,0:T(8,128)(2,1)S(1)} %fusion), channel_id=1, source_target_pairs={{0,0},{1,32},{2,128},{3,160},{4,4},{5,36},{6,132},{7,164},{8,256},... | collective-permute-start | bytes 110600 | tf_op jit(solution)/shard_map/ppermute | solution.py:68
  74.0 0.8 copy-start.1
  104.1 11.1 %collective-permute-start.2 = (bf16[12,2,72,128]{3,2,1,0:T(8,128)(2,1)S(1)}, bf16[12,2,72,128]{3,2,1,0:T(8,128)(2,1)S(1)}, u32[]{:S(2)}, u32[]{:S(2)}) collective-permute-start(bf16[12,2,72,128]{3,2,1,0:T(8,128)(2,1)S(1)} %all_to_all.20), channel_id=1, source_target_pairs={{0,8},{8,0},{1,9},{9,1},{2,10},{10,2},{3,11},{11,3},{4,12},{12,4},... | collective-permute-start | bytes 1327112 | tf_op jit(solution)/shard_map/ppermute | solution.py:73
  145.8 0.7 copy-start.5

commit v3 on v2

v3 whole, which is shorter than its diff:
```python
import numpy as np
import jax
import jax.numpy as jnp
from jax import lax
from jax.experimental import pallas as pl
from jax.sharding import Mesh, PartitionSpec as P

LAYERS = 2
AXES = ("za", "zb", "ya", "yb", "core", "yhi", "x")
SIZES = (6, 2, 2, 2, 2, 2, 4)
NX = 4
N_OWNER = 8
BLK = ("za", "zb", "ya", "yb", "core")
OWNER = ("yhi", "x")
CHUNK = ("zb", "yb", "x")
N_CHUNK = 16
N_ROWS = 4
BLOCKS = 6
FLIP = [(0, 1), (1, 0)]


def spread_pairs(flip):
    source = np.arange(np.prod(SIZES)).reshape(SIZES)
    pairs = []
    for za, zb, ya, yb, core, yhi, x in np.ndindex(*SIZES):
        target = source[za, zb, (x // 2) ^ flip, yb, x % 2, yhi, 2 * ya + core]
        pairs.append((int(source[za, zb, ya, yb, core, yhi, x]), int(target)))
    return pairs


def copies(value, axis, count):
    return lax.all_to_all(jnp.broadcast_to(value[None], (count,) + value.shape), axis, 0, 0)


def ordered(mine, other, axis):
    first = lax.axis_index(axis) == 0
    return jnp.stack([jnp.where(first, mine, other), jnp.where(first, other, mine)])


def chunk_kernel(factor_ref, chunks_ref):
    rows = factor_ref.shape[1]
    for zb, yb, ya, core in np.ndindex(2, 2, 2, 2):
        at = ((zb * 2 + ya) * 2 + yb) * 2 + core
        runs = [
            factor_ref[0, :, (za * N_CHUNK + at) * rows : (za * N_CHUNK + at + 1) * rows]
            for za in range(BLOCKS)
        ]
        chunks_ref[((zb * 2 + yb) * 2 + ya) * 2 + core] = jnp.concatenate(runs, axis=1)


def column_chunks(factor):
    _, rows, width = factor.shape
    return pl.pallas_call(
        chunk_kernel,
        out_shape=jax.ShapeDtypeStruct((N_CHUNK, rows, width // N_CHUNK), factor.dtype),
        cost_estimate=pl.CostEstimate(
            flops=0, bytes_accessed=4 * rows * width, transcendentals=0
        ),
    )(factor)


def body(grad_blocks, ginv_factors, ainv_owned, owner_table, damp_grad, damp_act):
    rows, cols = grad_blocks.shape[1:]
    width = ainv_owned.shape[2] // N_CHUNK
    yhi = lax.axis_index("yhi")

    gathered = copies(grad_blocks, OWNER, N_OWNER)
    gathered = gathered.transpose(1, 2, 0, 3).reshape(LAYERS, rows, N_OWNER * cols)
    right = lax.dot_general(
        gathered, ginv_factors, (((2,), (1,)), ((0,), (0,))), preferred_element_type=jnp.float32
    )
    right = right + damp_grad[:, None, None] * grad_blocks.astype(jnp.float32)
    right = right.astype(jnp.bfloat16)
    near = lax.ppermute(right, AXES, spread_pairs(0))
    far = lax.ppermute(right, AXES, spread_pairs(1))
    piece = ordered(near, far, "ya")

    factor = column_chunks(ainv_owned)
    factor = lax.all_to_all(factor, CHUNK, 0, 0).reshape(N_ROWS, NX, rows, width)
    owner_half = owner_table // NX
    mine = jnp.stack(
        [
            lax.dynamic_index_in_dim(factor, owner_table[l] % NX, 1, keepdims=False)
            for l in range(LAYERS)
        ]
    ).reshape(LAYERS, N_ROWS * rows, width)
    mine, piece = lax.optimization_barrier((mine, piece))
    other = lax.ppermute(mine, "yhi", FLIP)

    along = copies(piece, "za", BLOCKS)
    along, other = lax.optimization_barrier((along, other))
    factor = jnp.where((owner_half == yhi)[:, None, None], mine, other)
    chunk = ordered(along, lax.ppermute(along, "core", FLIP), "core")
    chunk = chunk.transpose(3, 1, 4, 2, 0, 5).reshape(LAYERS, BLOCKS * rows, NX * cols)

    partial = lax.dot_general(
        factor, chunk, (((2,), (1,)), ((0,), (0,))), preferred_element_type=jnp.float32
    )
    partial = partial.reshape(LAYERS, N_ROWS, rows, NX, cols).transpose(1, 3, 0, 2, 4)
    partial = partial.reshape(N_CHUNK, LAYERS, rows, cols)
    act = jnp.sum(lax.all_to_all(partial, CHUNK, 0, 0), axis=0)
    act = act + damp_act[:, None, None] * right.astype(jnp.float32)
    return act.astype(jnp.bfloat16)


def solution(mesh):
    fine = Mesh(mesh.devices.reshape(SIZES), AXES)
    return jax.shard_map(
        body,
        mesh=fine,
        in_specs=(
            P(None, BLK, OWNER),
            P(None, None, OWNER),
            P(OWNER, BLK, None),
            P(),
            P(),
            P(),
        ),
        out_specs=P(None, BLK, OWNER),
        check_vma=False,
    )
```

time: 148 us -> 126 us (0.85)
  blocking collectives: 56.9 us -> 31.4 us
  waiting for transfers between devices: 22.1 us -> 32.2 us
  starting transfers between devices: 51.6 us -> 46.6 us
  local copies, waits for them, and re-layouts: 10.1 us -> 5.45 us
  Pallas kernels: 0 us -> 3.01 us
    all_to_all x1 -> x0, blocking collectives: 29.2 us -> none  [copies(): lax.all_to_all(jnp.broadcast_to(value[None], (count,) + value.shape), axi...]
    ppermute x3 -> x4, starting transfers between devices: 33.1 us -> 13.9 us  [the longest x1 5.3 us: body(): chunk = ordered(along, lax.ppermute(along, 'core', FLIP), 'core')]
    all_to_all x1 -> x2, starting transfers between devices: 10.5 us -> 24 us  [copies(): lax.all_to_all(jnp.broadcast_to(value[None], (count,) + value.shape), axi...]
    ppermute x3 -> x4, waiting for transfers between devices: 10.6 us -> 23.6 us  [the longest x1 18 us: body(): other = lax.ppermute(mine, 'yhi', FLIP)]
    all_to_all x1, waiting for transfers between devices: 8.58 us -> 1.46 us  [body(): lax.all_to_all(factor, CHUNK, 0, 0).reshape(N_ROWS, NX, rows, width)]
    all_to_all x1 -> x2, waiting for transfers between devices: 2.87 us -> 7.2 us  [copies(): lax.all_to_all(jnp.broadcast_to(value[None], (count,) + value.shape), axi...]
    another operation x1 -> x0, local copies, waits for them, and re-layouts: 3.81 us -> none  [body(): factor = ainv_owned[0].reshape(rows, N_CHUNK, width).transpose(1, 0, 2)]
    all_to_all x1, blocking collectives: 27.7 us -> 31.4 us  [body(): act = jnp.sum(lax.all_to_all(partial, CHUNK, 0, 0), axis=0)]
  transfers between devices with their start and end apart: 5 -> 7, of which waited for: 4 -> 6; matrix products, arithmetic and copies ran while one was open for 1% -> 1% of each run, Pallas kernels for 0% -> 2%
where the time goes in v3:
time: 126 us
  starting transfers between devices  46.6 us (37%)
  waiting for transfers between devices  32.2 us (26%)
  blocking collectives  31.4 us (25%)
  local copies, waits for them, and re-layouts  5.45 us (4%)
  between operations  4.06 us (3%)
  Pallas kernels  3.01 us (2%)
  matrix products  1.8 us (1%)
    all_to_all x1, blocking collectives, body(): act = jnp.sum(lax.all_to_all(partial, CHUNK, 0, 0), axis=0)  31.4 us
    all_to_all x2, starting transfers between devices, copies(): lax.all_to_all(jnp.broadcast_to(value[None], (count,) + value.shape), axi...  24 us
    ppermute x1, waiting for transfers between devices, body(): other = lax.ppermute(mine, 'yhi', FLIP)  18 us
    all_to_all x1, starting transfers between devices, body(): lax.all_to_all(factor, CHUNK, 0, 0).reshape(N_ROWS, NX, rows, width)  8.58 us
    all_to_all x2, waiting for transfers between devices, copies(): lax.all_to_all(jnp.broadcast_to(value[None], (count,) + value.shape), axi...  7.2 us
    ppermute x1, starting transfers between devices, body(): chunk = ordered(along, lax.ppermute(along, 'core', FLIP), 'core')  5.3 us
    ppermute x1, starting transfers between devices, body(): far = lax.ppermute(right, AXES, spread_pairs(1))  4.55 us
    ppermute x1, waiting for transfers between devices, body(): far = lax.ppermute(right, AXES, spread_pairs(1))  4.15 us
  transfers between devices with their start and end apart: 7, of which 6 were waited for; matrix products, arithmetic and copies ran while one was open for 1% of the time, Pallas kernels for 2%

profile of v3, /device:TPU:1, one launch (start us, length us, event | category | flops | bytes accessed | tf_op | source)
XLA Modules:
  0.0 125.5 jit_solution(3554884237634159284)
XLA Ops:
  0.0 0.0 copy-start
  0.0 1.6 %broadcast_in_dim.10 = bf16[8,2,72,128]{3,2,1,0:T(8,128)(2,1)} broadcast(bf16[2,72,128]{2,1,0:T(8,128)(2,1)} %param.6), dimensions={1,2,3} | broadcast | bytes 331776 | tf_op jit(solution)/shard_map/broadcast_in_dim | solution.py:32
  1.6 10.1 %all-to-all-start.1 = ((bf16[8,2,72,128]{3,2,1,0:T(8,128)(2,1)}), bf16[8,2,72,128]{3,2,1,0:T(8,128)(2,1)S(1)}, u32[]{:S(2)}, u32[]{:S(2)}) async-start(bf16[8,2,72,128]{3,2,1,0:T(8,128)(2,1)} %broadcast_in_dim.10), calls=%async_computation.1 | async-start | bytes 589824 | tf_op jit(solution)/shard_map/all_to_all | solution.py:32
  11.7 3.0 %shard_map.64 = bf16[16,72,432]{2,1,0:T(8,128)(2,1)} custom-call(bf16[1,72,6912]{2,1,0:T(8,128)(2,1)} %factor_ref.1), custom_call_target="tpu_custom_call" | custom-call | bytes 1990656 | tf_op jit(solution)/shard_map/pallas_call | solution.py:53
  14.7 0.0 copy-start.1
  14.7 0.0 copy-start.3
  14.7 0.0 copy-start.2
  14.7 7.2 %all-to-all-done.1 = bf16[8,2,72,128]{3,2,1,0:T(8,128)(2,1)S(1)} async-done(((bf16[8,2,72,128]{3,2,1,0:T(8,128)(2,1)}), bf16[8,2,72,128]{3,2,1,0:T(8,128)(2,1)S(1)}, u32[]{:S(2)}, u32[]{:S(2)}) %all-to-all-start.1) | async-done | bytes 294944 | tf_op jit(solution)/shard_map/all_to_all | solution.py:32
  21.9 8.6 %all-to-all-start = ((bf16[16,72,432]{2,1,0:T(8,128)(2,1)}), bf16[16,72,432]{2,1,0:T(8,128)(2,1)S(1)}, u32[]{:S(2)}, u32[]{:S(2)}) async-start(bf16[16,72,432]{2,1,0:T(8,128)(2,1)} %shard_map.64), calls=%async_computation | async-start | bytes 2359296 | tf_op jit(solution)/shard_map/all_to_all | solution.py:79
  30.5 0.0 copy-done
  30.5 0.0 copy-done.1
  30.5 0.0 copy-done.3
  30.5 0.2 fusion
  30.8 4.6 %collective-permute-start.1 = (bf16[2,72,128]{2,1,0:T(8,128)(2,1)S(1)}, bf16[2,72,128]{2,1,0:T(8,128)(2,1)S(1)}, u32[]{:S(2)}, u32[]{:S(2)}) collective-permute-start(bf16[2,72,128]{2,1,0:T(8,128)(2,1)S(1)} %fusion), channel_id=1, source_target_pairs={{0,32},{1,40},{2,0},{3,8},{4,36},{5,44},{6,4},{7,12},{8,33},{9,41}... | collective-permute-start | bytes 110600 | tf_op jit(solution)/shard_map/ppermute | solution.py:75
  35.3 1.9 %collective-permute-start = (bf16[2,72,128]{2,1,0:T(8,128)(2,1)S(1)}, bf16[2,72,128]{2,1,0:T(8,128)(2,1)S(1)}, u32[]{:S(2)}, u32[]{:S(2)}) collective-permute-start(bf16[2,72,128]{2,1,0:T(8,128)(2,1)S(1)} %fusion), channel_id=1, source_target_pairs={{0,0},{1,8},{2,32},{3,40},{4,4},{5,12},{6,36},{7,44},{8,1},{9,9},{... | collective-permute-start | bytes 110600 | tf_op jit(solution)/shard_map/ppermute | solution.py:74
  37.3 0.0 copy-done.2
  37.3 0.6 fusion.7
  41.8 4.1 %collective-permute-done.1 = bf16[2,72,128]{2,1,0:T(8,128)(2,1)S(1)} collective-permute-done((bf16[2,72,128]{2,1,0:T(8,128)(2,1)S(1)}, bf16[2,72,128]{2,1,0:T(8,128)(2,1)S(1)}, u32[]{:S(2)}, u32[]{:S(2)}) %collective-permute-start.1) | collective-permute-done | bytes 36896 | tf_op jit(solution)/shard_map/ppermute | solution.py:75
  46.0 0.1 collective-permute-done
  46.1 1.5 %all-to-all-done = bf16[16,72,432]{2,1,0:T(8,128)(2,1)S(1)} async-done(((bf16[16,72,432]{2,1,0:T(8,128)(2,1)}), bf16[16,72,432]{2,1,0:T(8,128)(2,1)S(1)}, u32[]{:S(2)}, u32[]{:S(2)}) %all-to-all-start) | async-done | bytes 995360 | tf_op jit(solution)/shard_map/all_to_all | solution.py:79
  47.6 0.1 pad_maximum_fusion
  47.6 0.8 broadcast_in_dim.11
  48.5 13.9 %all-to-all-start.2 = ((bf16[6,2,2,72,128]{4,3,2,1,0:T(8,128)(2,1)}), bf16[6,2,2,72,128]{4,3,2,1,0:T(8,128)(2,1)S(1)}, u32[]{:S(2)}, u32[]{:S(2)}) async-start(bf16[6,2,2,72,128]{4,3,2,1,0:T(8,128)(2,1)} %broadcast_in_dim.11), calls=%async_computation.2 | async-start | bytes 884736 | tf_op jit(solution)/shard_map/all_to_all | solution.py:32
  62.4 2.2 %collective-permute-start.2 = (bf16[2,288,432]{2,1,0:T(8,128)(2,1)S(1)}, bf16[2,288,432]{2,1,0:T(8,128)(2,1)}, u32[]{:S(2)}, u32[]{:S(2)}) collective-permute-start(bf16[2,288,432]{2,1,0:T(8,128)(2,1)S(1)} %pad_maximum_fusion), channel_id=1, source_target_pairs={{0,4},{4,0},{1,5},{5,1},{2,6},{6,2},{3,7},{7,3},{8,12},{12,8},{9,1... | collective-permute-start | bytes 1493000 | tf_op jit(solution)/shard_map/ppermute | solution.py:88
  64.6 18.0 %collective-permute-done.2 = bf16[2,288,432]{2,1,0:T(8,128)(2,1)} collective-permute-done((bf16[2,288,432]{2,1,0:T(8,128)(2,1)S(1)}, bf16[2,288,432]{2,1,0:T(8,128)(2,1)}, u32[]{:S(2)}, u32[]{:S(2)}) %collective-permute-start.2) | collective-permute-done | bytes 497696 | tf_op jit(solution)/shard_map/ppermute | solution.py:88
  82.6 0.0 all-to-all-done.2
  82.6 5.3 %collective-permute-start.3 = (bf16[6,2,2,72,128]{4,3,2,1,0:T(8,128)(2,1)S(1)}, bf16[6,2,2,72,128]{4,3,2,1,0:T(8,128)(2,1)S(1)}, u32[]{:S(2)}, u32[]{:S(2)}) collective-permute-start(bf16[6,2,2,72,128]{4,3,2,1,0:T(8,128)(2,1)S(1)} %all-to-all-done.2), channel_id=1, source_target_pairs={{0,8},{8,0},{1,9},{9,1},{2,10},{10,2},{3,11},{11,3},{4,12},{12,4},... | collective-permute-start | bytes 1327112 | tf_op jit(solution)/shard_map/ppermute | solution.py:93
  87.9 1.4 %collective-permute-done.3 = bf16[6,2,2,72,128]{4,3,2,1,0:T(8,128)(2,1)S(1)} collective-permute-done((bf16[6,2,2,72,128]{4,3,2,1,0:T(8,128)(2,1)S(1)}, bf16[6,2,2,72,128]{4,3,2,1,0:T(8,128)(2,1)S(1)}, u32[]{:S(2)}, u32[]{:S(2)}) %collective-permute-start.3) | collective-permute-done | bytes 442400 | tf_op jit(solution)/shard_map/ppermute | solution.py:93
  89.3 0.1 select_bitcast_fusion.1
  89.4 0.1 maximum_bitcast_fusion
  89.5 0.9 copy.12
  90.4 0.3 reshape.29
  90.7 1.6 %fusion.1 = f32[2,288,512]{2,1,0:T(8,128)S(1)} fusion(bf16[2,432,512]{2,1,0:T(8,128)(2,1)S(1)} %reshape.29, bf16[2,288,432]{2,1,0:T(8,128)(2,1)S(1)} %pad_maximum_fusion, bf16[2,288,432]{2,1,0:T(8,128)(2,1)} %collective-permute-done.2, pred[2]{0:T(512)(128)(4,1)S(1)} %fusion.6), kind=kOutput, calls=%fused_computation.4 | convolution fusion | flops 255052800 | bytes 3059714 | tf_op jit(solution)/shard_map/dot_general | solution.py:96
  92.3 0.4 reshape.30
  92.7 0.1 copy.13
  92.8 31.4 %all_to_all.20 = f32[16,2,72,128]{3,2,1,0:T(8,128)S(1)} all-to-all(f32[16,2,72,128]{3,2,1,0:T(8,128)S(1)} %bitcast.28), channel_id=1, replica_groups=mesh['za'=6,'zb'=2,'ya'=2,'yb'=2,'core'=2,'yhi'=2,'x'=4] {'zb','yb','x'}, dimensions={0} | all-to-all | bytes 2359296 | tf_op jit(solution)/shard_map/all_to_all | solution.py:101
  124.2 0.0 copy-start.4
  124.2 0.1 reduce_sum.9
  124.3 0.6 copy-done.4
  124.9 0.7 add_convert_fusion
  (4 shorter events, 0.1 us)
Async XLA Ops:
  0.0 30.5 %copy-start = (bf16[2,1024,128]{2,1,0:T(8,128)(2,1)S(1)}, bf16[2,1024,128]{2,1,0:T(8,128)(2,1)}, u32[]{:S(2)}) copy-start(bf16[2,1024,128]{2,1,0:T(8,128)(2,1)} %param.7) | copy-start | bytes 1572868
  1.6 20.3 %all-to-all-start.1 = ((bf16[8,2,72,128]{3,2,1,0:T(8,128)(2,1)}), bf16[8,2,72,128]{3,2,1,0:T(8,128)(2,1)S(1)}, u32[]{:S(2)}, u32[]{:S(2)}) async-start(bf16[8,2,72,128]{3,2,1,0:T(8,128)(2,1)} %broadcast_in_dim.10), calls=%async_computation.1 | async-start | bytes 589824 | tf_op jit(solution)/shard_map/all_to_all | solution.py:32
  14.7 15.8 %copy-start.1 = (bf16[2,72,128]{2,1,0:T(8,128)(2,1)S(1)}, bf16[2,72,128]{2,1,0:T(8,128)(2,1)}, u32[]{:S(2)}) copy-start(bf16[2,72,128]{2,1,0:T(8,128)(2,1)} %param.6) | copy-start | bytes 110596
  14.7 15.8 %copy-start.3 = (f32[2]{0:T(128)S(1)}, f32[2]{0:T(128)}, u32[]{:S(2)}) copy-start(f32[2]{0:T(128)} %param.10) | copy-start | bytes 28
  14.7 22.6 %copy-start.2 = (s32[2]{0:T(128)S(1)}, s32[2]{0:T(128)}, u32[]{:S(2)}) copy-start(s32[2]{0:T(128)} %param.9) | copy-start | bytes 28
  21.9 25.6 %all-to-all-start = ((bf16[16,72,432]{2,1,0:T(8,128)(2,1)}), bf16[16,72,432]{2,1,0:T(8,128)(2,1)S(1)}, u32[]{:S(2)}, u32[]{:S(2)}) async-start(bf16[16,72,432]{2,1,0:T(8,128)(2,1)} %shard_map.64), calls=%async_computation | async-start | bytes 2359296 | tf_op jit(solution)/shard_map/all_to_all | solution.py:79
  30.8 15.2 %collective-permute-start.1 = (bf16[2,72,128]{2,1,0:T(8,128)(2,1)S(1)}, bf16[2,72,128]{2,1,0:T(8,128)(2,1)S(1)}, u32[]{:S(2)}, u32[]{:S(2)}) collective-permute-start(bf16[2,72,128]{2,1,0:T(8,128)(2,1)S(1)} %fusion), channel_id=1, source_target_pairs={{0,32},{1,40},{2,0},{3,8},{4,36},{5,44},{6,4},{7,12},{8,33},{9,41}... | collective-permute-start | bytes 110600 | tf_op jit(solution)/shard_map/ppermute | solution.py:75
  35.3 10.7 %collective-permute-start = (bf16[2,72,128]{2,1,0:T(8,128)(2,1)S(1)}, bf16[2,72,128]{2,1,0:T(8,128)(2,1)S(1)}, u32[]{:S(2)}, u32[]{:S(2)}) collective-permute-start(bf16[2,72,128]{2,1,0:T(8,128)(2,1)S(1)} %fusion), channel_id=1, source_target_pairs={{0,0},{1,8},{2,32},{3,40},{4,4},{5,12},{6,36},{7,44},{8,1},{9,9},{... | collective-permute-start | bytes 110600 | tf_op jit(solution)/shard_map/ppermute | solution.py:74
  48.5 34.1 %all-to-all-start.2 = ((bf16[6,2,2,72,128]{4,3,2,1,0:T(8,128)(2,1)}), bf16[6,2,2,72,128]{4,3,2,1,0:T(8,128)(2,1)S(1)}, u32[]{:S(2)}, u32[]{:S(2)}) async-start(bf16[6,2,2,72,128]{4,3,2,1,0:T(8,128)(2,1)} %broadcast_in_dim.11), calls=%async_computation.2 | async-start | bytes 884736 | tf_op jit(solution)/shard_map/all_to_all | solution.py:32
  62.4 20.2 %collective-permute-start.2 = (bf16[2,288,432]{2,1,0:T(8,128)(2,1)S(1)}, bf16[2,288,432]{2,1,0:T(8,128)(2,1)}, u32[]{:S(2)}, u32[]{:S(2)}) collective-permute-start(bf16[2,288,432]{2,1,0:T(8,128)(2,1)S(1)} %pad_maximum_fusion), channel_id=1, source_target_pairs={{0,4},{4,0},{1,5},{5,1},{2,6},{6,2},{3,7},{7,3},{8,12},{12,8},{9,1... | collective-permute-start | bytes 1493000 | tf_op jit(solution)/shard_map/ppermute | solution.py:88
  82.6 6.7 %collective-permute-start.3 = (bf16[6,2,2,72,128]{4,3,2,1,0:T(8,128)(2,1)S(1)}, bf16[6,2,2,72,128]{4,3,2,1,0:T(8,128)(2,1)S(1)}, u32[]{:S(2)}, u32[]{:S(2)}) collective-permute-start(bf16[6,2,2,72,128]{4,3,2,1,0:T(8,128)(2,1)S(1)} %all-to-all-done.2), channel_id=1, source_target_pairs={{0,8},{8,0},{1,9},{9,1},{2,10},{10,2},{3,11},{11,3},{4,12},{12,4},... | collective-permute-start | bytes 1327112 | tf_op jit(solution)/shard_map/ppermute | solution.py:93
  124.2 0.7 copy-start.4

commit v4 on v3

--- a/solution.py
+++ b/solution.py
@@ -78,18 +78,27 @@
     factor = column_chunks(ainv_owned)
     factor = lax.all_to_all(factor, CHUNK, 0, 0).reshape(N_ROWS, NX, rows, width)
     owner_half = owner_table // NX
-    mine = jnp.stack(
-        [
-            lax.dynamic_index_in_dim(factor, owner_table[l] % NX, 1, keepdims=False)
-            for l in range(LAYERS)
-        ]
-    ).reshape(LAYERS, N_ROWS * rows, width)
-    mine, piece = lax.optimization_barrier((mine, piece))
-    other = lax.ppermute(mine, "yhi", FLIP)
+    here = owner_half == yhi
+
+    def of_owner(owner):
+        part = lax.dynamic_index_in_dim(factor, owner % NX, 1, keepdims=False)
+        return part.reshape(N_ROWS * rows, width)
+
+    mine = [of_owner(owner_table[l]) for l in range(LAYERS)]
+    one_half = owner_half[0] == owner_half[1]
+    first = of_owner(jnp.where(here[0], owner_table[0], owner_table[1]))
+    first, piece = lax.optimization_barrier((first, piece))
+    first = lax.ppermute(first, "yhi", FLIP)
+    second = lax.cond(one_half, lambda part: lax.ppermute(part, "yhi", FLIP), lambda part: part, mine[1])
 
     along = copies(piece, "za", BLOCKS)
-    along, other = lax.optimization_barrier((along, other))
-    factor = jnp.where((owner_half == yhi)[:, None, None], mine, other)
+    along, first = lax.optimization_barrier((along, first))
+    factor = jnp.stack(
+        [
+            jnp.where(here[0], mine[0], first),
+            jnp.where(here[1], mine[1], jnp.where(one_half, second, first)),
+        ]
+    )
     chunk = ordered(along, lax.ppermute(along, "core", FLIP), "core")
     chunk = chunk.transpose(3, 1, 4, 2, 0, 5).reshape(LAYERS, BLOCKS * rows, NX * cols)
 

time: 126 us -> 138 us (1.095)
  waiting for transfers between devices: 32.2 us -> 39.3 us
  blocking collectives: 31.4 us -> 27.5 us
  between operations: 4.06 us -> 7.25 us
  other arithmetic: 1.01 us -> 3.15 us
  local copies, waits for them, and re-layouts: 5.45 us -> 7.48 us
    all_to_all x2, waiting for transfers between devices: 7.2 us -> 13.7 us  [copies(): lax.all_to_all(jnp.broadcast_to(value[None], (count,) + value.shape), axi...]
    ppermute x1 -> x2, waiting for transfers between devices: 18 us -> 22.4 us  [the longest x1 12.5 us: body(): lax.ppermute(part, 'yhi', FLIP)]
    all_to_all x1, blocking collectives: 31.4 us -> 27.5 us  [body(): act = jnp.sum(lax.all_to_all(partial, CHUNK, 0, 0), axis=0)]
    ppermute x1, waiting for transfers between devices: 4.15 us -> 1.72 us  [body(): far = lax.ppermute(right, AXES, spread_pairs(1))]
    select_n x0 -> x1, other arithmetic: none -> 2.21 us  [body(): jnp.where(here[0], mine[0], first)]
    ppermute x1 -> x2, starting transfers between devices: 2.18 us -> 4.37 us  [the longest x1 2.19 us: body(): lax.ppermute(part, 'yhi', FLIP)]
    ppermute x1, starting transfers between devices: 5.3 us -> 3.9 us  [body(): chunk = ordered(along, lax.ppermute(along, 'core', FLIP), 'core')]
  transfers between devices with their start and end apart: 7 -> 8, of which waited for: 6 -> 7; matrix products, arithmetic and copies ran while one was open for 1% -> 3% of each run, Pallas kernels for 2% -> 2%
where the time goes in v4:
time: 138 us; the launch traced here: 137 us
  starting transfers between devices  47.4 us (34%)
  waiting for transfers between devices  39.3 us (28%)
  blocking collectives  27.5 us (20%)
  local copies, waits for them, and re-layouts  7.48 us (5%)
  between operations  7.25 us (5%)
  other arithmetic  3.15 us (2%)
  Pallas kernels  3.02 us (2%)
  matrix products  1.87 us (1%)
    all_to_all x1, blocking collectives, body(): act = jnp.sum(lax.all_to_all(partial, CHUNK, 0, 0), axis=0)  27.5 us
    all_to_all x2, starting transfers between devices, copies(): lax.all_to_all(jnp.broadcast_to(value[None], (count,) + value.shape), axi...  24 us
    all_to_all x2, waiting for transfers between devices, copies(): lax.all_to_all(jnp.broadcast_to(value[None], (count,) + value.shape), axi...  13.7 us
    ppermute x1, waiting for transfers between devices, body(): lax.ppermute(part, 'yhi', FLIP)  12.5 us
    ppermute x1, waiting for transfers between devices, body(): first = lax.ppermute(first, 'yhi', FLIP)  9.87 us
    all_to_all x1, starting transfers between devices, body(): lax.all_to_all(factor, CHUNK, 0, 0).reshape(N_ROWS, NX, rows, width)  8.58 us
    ppermute x1, starting transfers between devices, body(): far = lax.ppermute(right, AXES, spread_pairs(1))  4.55 us
    ppermute x1, starting transfers between devices, body(): chunk = ordered(along, lax.ppermute(along, 'core', FLIP), 'core')  3.9 us
  transfers between devices with their start and end apart: 8, of which 7 were waited for; matrix products, arithmetic and copies ran while one was open for 3% of the time, Pallas kernels for 2%

profile of v4, /device:TPU:1, one launch (start us, length us, event | category | flops | bytes accessed | tf_op | source)
XLA Modules:
  0.0 137.0 jit_solution(4277959914978015058)
XLA Ops:
  0.0 0.0 copy-start
  0.0 1.6 %broadcast_in_dim.4 = bf16[8,2,72,128]{3,2,1,0:T(8,128)(2,1)} broadcast(bf16[2,72,128]{2,1,0:T(8,128)(2,1)} %param.8), dimensions={1,2,3} | broadcast | bytes 331776 | tf_op jit(solution)/shard_map/broadcast_in_dim | solution.py:32
  1.6 10.1 %all-to-all-start.1 = ((bf16[8,2,72,128]{3,2,1,0:T(8,128)(2,1)}), bf16[8,2,72,128]{3,2,1,0:T(8,128)(2,1)S(1)}, u32[]{:S(2)}, u32[]{:S(2)}) async-start(bf16[8,2,72,128]{3,2,1,0:T(8,128)(2,1)} %broadcast_in_dim.4), calls=%async_computation.1 | async-start | bytes 589824 | tf_op jit(solution)/shard_map/all_to_all | solution.py:32
  11.7 3.0 %shard_map.64 = bf16[16,72,432]{2,1,0:T(8,128)(2,1)} custom-call(bf16[1,72,6912]{2,1,0:T(8,128)(2,1)} %factor_ref.1), custom_call_target="tpu_custom_call" | custom-call | bytes 1990656 | tf_op jit(solution)/shard_map/pallas_call | solution.py:53
  14.7 0.0 copy-start.2
  14.7 0.0 copy-start.1
  14.7 0.0 copy-start.3
  14.7 7.2 %all-to-all-done.1 = bf16[8,2,72,128]{3,2,1,0:T(8,128)(2,1)S(1)} async-done(((bf16[8,2,72,128]{3,2,1,0:T(8,128)(2,1)}), bf16[8,2,72,128]{3,2,1,0:T(8,128)(2,1)S(1)}, u32[]{:S(2)}, u32[]{:S(2)}) %all-to-all-start.1) | async-done | bytes 294944 | tf_op jit(solution)/shard_map/all_to_all | solution.py:32
  21.9 8.6 %all-to-all-start = ((bf16[16,72,432]{2,1,0:T(8,128)(2,1)}), bf16[16,72,432]{2,1,0:T(8,128)(2,1)S(1)}, u32[]{:S(2)}, u32[]{:S(2)}) async-start(bf16[16,72,432]{2,1,0:T(8,128)(2,1)} %shard_map.64), calls=%async_computation | async-start | bytes 2359296 | tf_op jit(solution)/shard_map/all_to_all | solution.py:79
  30.5 0.0 copy-done.2
  30.5 0.6 fusion.8
  31.1 0.0 copy-done
  31.1 0.0 copy-done.1
  31.1 0.0 copy-done.3
  31.1 0.2 fusion
  31.4 4.5 %collective-permute-start.2 = (bf16[2,72,128]{2,1,0:T(8,128)(2,1)S(1)}, bf16[2,72,128]{2,1,0:T(8,128)(2,1)S(1)}, u32[]{:S(2)}, u32[]{:S(2)}) collective-permute-start(bf16[2,72,128]{2,1,0:T(8,128)(2,1)S(1)} %fusion), channel_id=1, source_target_pairs={{0,32},{1,40},{2,0},{3,8},{4,36},{5,44},{6,4},{7,12},{8,33},{9,41}... | collective-permute-start | bytes 110600 | tf_op jit(solution)/shard_map/ppermute | solution.py:75
  35.9 1.9 %collective-permute-start.1 = (bf16[2,72,128]{2,1,0:T(8,128)(2,1)S(1)}, bf16[2,72,128]{2,1,0:T(8,128)(2,1)S(1)}, u32[]{:S(2)}, u32[]{:S(2)}) collective-permute-start(bf16[2,72,128]{2,1,0:T(8,128)(2,1)S(1)} %fusion), channel_id=1, source_target_pairs={{0,0},{1,8},{2,32},{3,40},{4,4},{5,12},{6,36},{7,44},{8,1},{9,9},{... | collective-permute-start | bytes 110600 | tf_op jit(solution)/shard_map/ppermute | solution.py:74
  37.9 0.6 fusion.10
  44.2 1.7 %collective-permute-done.2 = bf16[2,72,128]{2,1,0:T(8,128)(2,1)S(1)} collective-permute-done((bf16[2,72,128]{2,1,0:T(8,128)(2,1)S(1)}, bf16[2,72,128]{2,1,0:T(8,128)(2,1)S(1)}, u32[]{:S(2)}, u32[]{:S(2)}) %collective-permute-start.2) | collective-permute-done | bytes 36896 | tf_op jit(solution)/shard_map/ppermute | solution.py:75
  46.0 0.1 collective-permute-done.1
  46.1 1.5 %all-to-all-done = bf16[16,72,432]{2,1,0:T(8,128)(2,1)S(1)} async-done(((bf16[16,72,432]{2,1,0:T(8,128)(2,1)}), bf16[16,72,432]{2,1,0:T(8,128)(2,1)S(1)}, u32[]{:S(2)}, u32[]{:S(2)}) %all-to-all-start) | async-done | bytes 995360 | tf_op jit(solution)/shard_map/all_to_all | solution.py:79
  47.5 0.1 constant_dynamic-slice_fusion.2
  47.6 0.8 broadcast_in_dim.5
  48.4 13.9 %all-to-all-start.2 = ((bf16[6,2,2,72,128]{4,3,2,1,0:T(8,128)(2,1)}), bf16[6,2,2,72,128]{4,3,2,1,0:T(8,128)(2,1)S(1)}, u32[]{:S(2)}, u32[]{:S(2)}) async-start(bf16[6,2,2,72,128]{4,3,2,1,0:T(8,128)(2,1)} %broadcast_in_dim.5), calls=%async_computation.2 | async-start | bytes 884736 | tf_op jit(solution)/shard_map/all_to_all | solution.py:32
  62.3 2.2 %collective-permute-start.3 = (bf16[288,432]{1,0:T(8,128)(2,1)S(1)}, bf16[288,432]{1,0:T(8,128)(2,1)S(1)}, u32[]{:S(2)}, u32[]{:S(2)}) collective-permute-start(bf16[288,432]{1,0:T(8,128)(2,1)S(1)} %bitcast.42), channel_id=1, source_target_pairs={{0,4},{4,0},{1,5},{5,1},{2,6},{6,2},{3,7},{7,3},{8,12},{12,8},{9,1... | collective-permute-start | bytes 746504 | tf_op jit(solution)/shard_map/ppermute | solution.py:91
  64.5 9.9 %collective-permute-done.3 = bf16[288,432]{1,0:T(8,128)(2,1)S(1)} collective-permute-done((bf16[288,432]{1,0:T(8,128)(2,1)S(1)}, bf16[288,432]{1,0:T(8,128)(2,1)S(1)}, u32[]{:S(2)}, u32[]{:S(2)}) %collective-permute-start.3) | collective-permute-done | bytes 248864 | tf_op jit(solution)/shard_map/ppermute | solution.py:91
  74.4 6.5 %all-to-all-done.2 = bf16[6,2,2,72,128]{4,3,2,1,0:T(8,128)(2,1)S(1)} async-done(((bf16[6,2,2,72,128]{4,3,2,1,0:T(8,128)(2,1)}), bf16[6,2,2,72,128]{4,3,2,1,0:T(8,128)(2,1)S(1)}, u32[]{:S(2)}, u32[]{:S(2)}) %all-to-all-start.2) | async-done | bytes 442400 | tf_op jit(solution)/shard_map/all_to_all | solution.py:32
  80.9 3.9 %collective-permute-start.4 = (bf16[6,2,2,72,128]{4,3,2,1,0:T(8,128)(2,1)S(1)}, bf16[6,2,2,72,128]{4,3,2,1,0:T(8,128)(2,1)S(1)}, u32[]{:S(2)}, u32[]{:S(2)}) collective-permute-start(bf16[6,2,2,72,128]{4,3,2,1,0:T(8,128)(2,1)S(1)} %all-to-all-done.2), channel_id=1, source_target_pairs={{0,8},{8,0},{1,9},{9,1},{2,10},{10,2},{3,11},{11,3},{4,12},{12,4},... | collective-permute-start | bytes 1327112 | tf_op jit(solution)/shard_map/ppermute | solution.py:102
  84.8 0.6 fusion.9
  86.7 14.7 %conditional.1 = (bf16[288,432]{1,0:T(8,128)(2,1)}) conditional(s32[]{:T(128)} %convert_element_type.17, bf16[288,432]{1,0:T(8,128)(2,1)S(1)} %bitcast.39, bf16[288,432]{1,0:T(8,128)(2,1)S(1)} %bitcast.40), branch_computations={%region_0.1_spmd, %region_1.2_spmd} | conditional | bytes 995376 | solution.py:92
  86.7 2.2 %collective-permute-start = (bf16[288,432]{1,0:T(8,128)(2,1)S(1)}, bf16[288,432]{1,0:T(8,128)(2,1)}, u32[]{:S(2)}, u32[]{:S(2)}) collective-permute-start(bf16[288,432]{1,0:T(8,128)(2,1)S(1)} %param.1), channel_id=1, source_target_pairs={{0,4},{4,0},{1,5},{5,1},{2,6},{6,2},{3,7},{7,3},{8,12},{12,8},{9,1... | collective-permute-start | bytes 746504 | tf_op jit(solution)/shard_map/cond/branch_1_fun/ppermute | solution.py:92
  88.9 12.5 %collective-permute-done = bf16[288,432]{1,0:T(8,128)(2,1)} collective-permute-done((bf16[288,432]{1,0:T(8,128)(2,1)S(1)}, bf16[288,432]{1,0:T(8,128)(2,1)}, u32[]{:S(2)}, u32[]{:S(2)}) %collective-permute-start) | collective-permute-done | bytes 248864 | tf_op jit(solution)/shard_map/cond/branch_1_fun/ppermute | solution.py:92
  101.4 2.2 %bitcast_select_fusion = (bf16[288,432]{1,0:T(8,128)(2,1)S(1)}, bf16[1,288,432]{2,1,0:T(8,128)(2,1)S(1)}) fusion(bf16[288,432]{1,0:T(8,128)(2,1)S(1)} %collective-permute-done.3, bf16[4,1,72,432]{3,2,1,0:T(8,128)(2,1)S(1)} %get-tuple-element.20, pred[]{:T(512)} %bitcast, bf16[288,432]{1,0:T(8,128)(2,1)} %get-tuple-element.35, pred[]{:T(512)} %bitcast.12, ...), kind=kLoop, calls=%fused_computation.11 | loop fusion | flops 373248 | bytes 1492995 | tf_op jit(solution)/shard_map/jit(_where)/select_n | solution.py:98
  103.6 0.0 collective-permute-done.4
  103.6 0.1 select_bitcast_fusion.1
  103.7 0.1 maximum_bitcast_fusion
  103.8 0.9 copy.12
  104.7 1.3 reshape.43
  105.9 1.6 %fusion.1 = f32[2,288,512]{2,1,0:T(8,128)S(1)} fusion(bf16[2,432,512]{2,1,0:T(8,128)(2,1)} %reshape.43, bf16[1,288,432]{2,1,0:T(8,128)(2,1)S(1)} %get-tuple-element.26, bf16[1,288,432]{2,1,0:T(8,128)(2,1)S(1)} %bitcast.41), kind=kOutput, calls=%fused_computation.3 | convolution fusion | flops 255052800 | bytes 2562048 | tf_op jit(solution)/shard_map/dot_general | solution.py:105
  107.6 0.4 reshape.44
  108.0 0.1 copy.13
  108.1 27.5 %all_to_all.20 = f32[16,2,72,128]{3,2,1,0:T(8,128)S(1)} all-to-all(f32[16,2,72,128]{3,2,1,0:T(8,128)S(1)} %bitcast.37), channel_id=1, replica_groups=mesh['za'=6,'zb'=2,'ya'=2,'yb'=2,'core'=2,'yhi'=2,'x'=4] {'zb','yb','x'}, dimensions={0} | all-to-all | bytes 2359296 | tf_op jit(solution)/shard_map/all_to_all | solution.py:110
  135.6 0.0 copy-start.4
  135.6 0.1 reduce_sum.9
  135.7 0.6 copy-done.4
  136.3 0.7 add_convert_fusion
  (3 shorter events, 0.0 us)
Async XLA Ops:
  0.0 31.1 %copy-start = (bf16[2,1024,128]{2,1,0:T(8,128)(2,1)S(1)}, bf16[2,1024,128]{2,1,0:T(8,128)(2,1)}, u32[]{:S(2)}) copy-start(bf16[2,1024,128]{2,1,0:T(8,128)(2,1)} %param.9) | copy-start | bytes 1572868
  1.6 20.3 %all-to-all-start.1 = ((bf16[8,2,72,128]{3,2,1,0:T(8,128)(2,1)}), bf16[8,2,72,128]{3,2,1,0:T(8,128)(2,1)S(1)}, u32[]{:S(2)}, u32[]{:S(2)}) async-start(bf16[8,2,72,128]{3,2,1,0:T(8,128)(2,1)} %broadcast_in_dim.4), calls=%async_computation.1 | async-start | bytes 589824 | tf_op jit(solution)/shard_map/all_to_all | solution.py:32
  14.7 15.8 %copy-start.2 = (s32[2]{0:T(128)S(1)}, s32[2]{0:T(128)}, u32[]{:S(2)}) copy-start(s32[2]{0:T(128)} %param.11) | copy-start | bytes 28
  14.7 16.4 %copy-start.1 = (bf16[2,72,128]{2,1,0:T(8,128)(2,1)S(1)}, bf16[2,72,128]{2,1,0:T(8,128)(2,1)}, u32[]{:S(2)}) copy-start(bf16[2,72,128]{2,1,0:T(8,128)(2,1)} %param.8) | copy-start | bytes 110596
  14.7 16.4 %copy-start.3 = (f32[2]{0:T(128)S(1)}, f32[2]{0:T(128)}, u32[]{:S(2)}) copy-start(f32[2]{0:T(128)} %param.12) | copy-start | bytes 28
  21.9 25.6 %all-to-all-start = ((bf16[16,72,432]{2,1,0:T(8,128)(2,1)}), bf16[16,72,432]{2,1,0:T(8,128)(2,1)S(1)}, u32[]{:S(2)}, u32[]{:S(2)}) async-start(bf16[16,72,432]{2,1,0:T(8,128)(2,1)} %shard_map.64), calls=%async_computation | async-start | bytes 2359296 | tf_op jit(solution)/shard_map/all_to_all | solution.py:79
  31.4 14.6 %collective-permute-start.2 = (bf16[2,72,128]{2,1,0:T(8,128)(2,1)S(1)}, bf16[2,72,128]{2,1,0:T(8,128)(2,1)S(1)}, u32[]{:S(2)}, u32[]{:S(2)}) collective-permute-start(bf16[2,72,128]{2,1,0:T(8,128)(2,1)S(1)} %fusion), channel_id=1, source_target_pairs={{0,32},{1,40},{2,0},{3,8},{4,36},{5,44},{6,4},{7,12},{8,33},{9,41}... | collective-permute-start | bytes 110600 | tf_op jit(solution)/shard_map/ppermute | solution.py:75
  35.9 10.1 %collective-permute-start.1 = (bf16[2,72,128]{2,1,0:T(8,128)(2,1)S(1)}, bf16[2,72,128]{2,1,0:T(8,128)(2,1)S(1)}, u32[]{:S(2)}, u32[]{:S(2)}) collective-permute-start(bf16[2,72,128]{2,1,0:T(8,128)(2,1)S(1)} %fusion), channel_id=1, source_target_pairs={{0,0},{1,8},{2,32},{3,40},{4,4},{5,12},{6,36},{7,44},{8,1},{9,9},{... | collective-permute-start | bytes 110600 | tf_op jit(solution)/shard_map/ppermute | solution.py:74
  48.4 32.5 %all-to-all-start.2 = ((bf16[6,2,2,72,128]{4,3,2,1,0:T(8,128)(2,1)}), bf16[6,2,2,72,128]{4,3,2,1,0:T(8,128)(2,1)S(1)}, u32[]{:S(2)}, u32[]{:S(2)}) async-start(bf16[6,2,2,72,128]{4,3,2,1,0:T(8,128)(2,1)} %broadcast_in_dim.5), calls=%async_computation.2 | async-start | bytes 884736 | tf_op jit(solution)/shard_map/all_to_all | solution.py:32
  62.3 12.1 %collective-permute-start.3 = (bf16[288,432]{1,0:T(8,128)(2,1)S(1)}, bf16[288,432]{1,0:T(8,128)(2,1)S(1)}, u32[]{:S(2)}, u32[]{:S(2)}) collective-permute-start(bf16[288,432]{1,0:T(8,128)(2,1)S(1)} %bitcast.42), channel_id=1, source_target_pairs={{0,4},{4,0},{1,5},{5,1},{2,6},{6,2},{3,7},{7,3},{8,12},{12,8},{9,1... | collective-permute-start | bytes 746504 | tf_op jit(solution)/shard_map/ppermute | solution.py:91
  80.9 22.7 %collective-permute-start.4 = (bf16[6,2,2,72,128]{4,3,2,1,0:T(8,128)(2,1)S(1)}, bf16[6,2,2,72,128]{4,3,2,1,0:T(8,128)(2,1)S(1)}, u32[]{:S(2)}, u32[]{:S(2)}) collective-permute-start(bf16[6,2,2,72,128]{4,3,2,1,0:T(8,128)(2,1)S(1)} %all-to-all-done.2), channel_id=1, source_target_pairs={{0,8},{8,0},{1,9},{9,1},{2,10},{10,2},{3,11},{11,3},{4,12},{12,4},... | collective-permute-start | bytes 1327112 | tf_op jit(solution)/shard_map/ppermute | solution.py:102
  86.7 14.7 %collective-permute-start = (bf16[288,432]{1,0:T(8,128)(2,1)S(1)}, bf16[288,432]{1,0:T(8,128)(2,1)}, u32[]{:S(2)}, u32[]{:S(2)}) collective-permute-start(bf16[288,432]{1,0:T(8,128)(2,1)S(1)} %param.1), channel_id=1, source_target_pairs={{0,4},{4,0},{1,5},{5,1},{2,6},{6,2},{3,7},{7,3},{8,12},{12,8},{9,1... | collective-permute-start | bytes 746504 | tf_op jit(solution)/shard_map/cond/branch_1_fun/ppermute | solution.py:92
  135.6 0.7 copy-start.4

commit v5 on v4

--- a/solution.py
+++ b/solution.py
@@ -106,8 +106,8 @@
         factor, chunk, (((2,), (1,)), ((0,), (0,))), preferred_element_type=jnp.float32
     )
     partial = partial.reshape(LAYERS, N_ROWS, rows, NX, cols).transpose(1, 3, 0, 2, 4)
-    partial = partial.reshape(N_CHUNK, LAYERS, rows, cols)
-    act = jnp.sum(lax.all_to_all(partial, CHUNK, 0, 0), axis=0)
+    partial = partial.reshape(N_CHUNK, LAYERS, rows, cols).astype(jnp.bfloat16)
+    act = jnp.sum(lax.all_to_all(partial, CHUNK, 0, 0).astype(jnp.float32), axis=0)
     act = act + damp_act[:, None, None] * right.astype(jnp.float32)
     return act.astype(jnp.bfloat16)
 

time: 138 us -> 108 us (0.78)
  waiting for transfers between devices: 39.3 us -> 24.8 us
  blocking collectives: 27.5 us -> 16.1 us
    ppermute x1 -> x0, waiting for transfers between devices: 12.5 us -> none  [body(): lax.ppermute(part, 'yhi', FLIP)]
    all_to_all x1, blocking collectives: 27.5 us -> 16.1 us  [body(): lax.all_to_all(partial, CHUNK, 0, 0).astype(jnp.float32)]
    ppermute x1, starting transfers between devices: 1.92 us -> 4.43 us  [body(): near = lax.ppermute(right, AXES, spread_pairs(0))]
    ppermute x1 -> x0, starting transfers between devices: 2.19 us -> none  [body(): lax.ppermute(part, 'yhi', FLIP)]
    ppermute x1, waiting for transfers between devices: 1.72 us -> 0.01 us  [body(): far = lax.ppermute(right, AXES, spread_pairs(1))]
  transfers between devices with their start and end apart: 8 -> 7, of which waited for: 7 -> 5; matrix products, arithmetic and copies ran while one was open for 3% -> 4% of each run, Pallas kernels for 2% -> 3%
where the time goes in v5:
time: 108 us
  starting transfers between devices  47.1 us (44%)
  waiting for transfers between devices  24.8 us (23%)
  blocking collectives  16.1 us (15%)
  between operations  7.27 us (7%)
  local copies, waits for them, and re-layouts  6.41 us (6%)
  Pallas kernels  3.02 us (3%)
  other arithmetic  2.23 us (2%)
    all_to_all x2, starting transfers between devices, copies(): lax.all_to_all(jnp.broadcast_to(value[None], (count,) + value.shape), axi...  24 us
    all_to_all x1, blocking collectives, body(): lax.all_to_all(partial, CHUNK, 0, 0).astype(jnp.float32)  16.1 us
    all_to_all x2, waiting for transfers between devices, copies(): lax.all_to_all(jnp.broadcast_to(value[None], (count,) + value.shape), axi...  13.7 us
    ppermute x1, waiting for transfers between devices, body(): first = lax.ppermute(first, 'yhi', FLIP)  9.87 us
    all_to_all x1, starting transfers between devices, body(): lax.all_to_all(factor, CHUNK, 0, 0).reshape(N_ROWS, NX, rows, width)  8.58 us
    ppermute x1, starting transfers between devices, body(): near = lax.ppermute(right, AXES, spread_pairs(0))  4.43 us
    ppermute x1, starting transfers between devices, body(): far = lax.ppermute(right, AXES, spread_pairs(1))  4 us
    ppermute x1, starting transfers between devices, body(): chunk = ordered(along, lax.ppermute(along, 'core', FLIP), 'core')  3.9 us
  transfers between devices with their start and end apart: 7, of which 5 were waited for; matrix products, arithmetic and copies ran while one was open for 4% of the time, Pallas kernels for 3%

profile of v5, /device:TPU:1, one launch (start us, length us, event | category | flops | bytes accessed | tf_op | source)
XLA Modules:
  0.0 107.8 jit_solution(16697541353639197334)
XLA Ops:
  0.0 0.0 copy-start
  0.0 1.6 %broadcast_in_dim.4 = bf16[8,2,72,128]{3,2,1,0:T(8,128)(2,1)} broadcast(bf16[2,72,128]{2,1,0:T(8,128)(2,1)} %param.8), dimensions={1,2,3} | broadcast | bytes 331776 | tf_op jit(solution)/shard_map/broadcast_in_dim | solution.py:32
  1.6 10.1 %all-to-all-start.1 = ((bf16[8,2,72,128]{3,2,1,0:T(8,128)(2,1)}), bf16[8,2,72,128]{3,2,1,0:T(8,128)(2,1)S(1)}, u32[]{:S(2)}, u32[]{:S(2)}) async-start(bf16[8,2,72,128]{3,2,1,0:T(8,128)(2,1)} %broadcast_in_dim.4), calls=%async_computation.1 | async-start | bytes 589824 | tf_op jit(solution)/shard_map/all_to_all | solution.py:32
  11.7 3.0 %shard_map.64 = bf16[16,72,432]{2,1,0:T(8,128)(2,1)} custom-call(bf16[1,72,6912]{2,1,0:T(8,128)(2,1)} %factor_ref.1), custom_call_target="tpu_custom_call" | custom-call | bytes 1990656 | tf_op jit(solution)/shard_map/pallas_call | solution.py:53
  14.7 0.0 copy-start.2
  14.7 0.0 copy-start.1
  14.7 0.0 copy-start.3
  14.7 7.2 %all-to-all-done.1 = bf16[8,2,72,128]{3,2,1,0:T(8,128)(2,1)S(1)} async-done(((bf16[8,2,72,128]{3,2,1,0:T(8,128)(2,1)}), bf16[8,2,72,128]{3,2,1,0:T(8,128)(2,1)S(1)}, u32[]{:S(2)}, u32[]{:S(2)}) %all-to-all-start.1) | async-done | bytes 294944 | tf_op jit(solution)/shard_map/all_to_all | solution.py:32
  21.9 8.6 %all-to-all-start = ((bf16[16,72,432]{2,1,0:T(8,128)(2,1)}), bf16[16,72,432]{2,1,0:T(8,128)(2,1)S(1)}, u32[]{:S(2)}, u32[]{:S(2)}) async-start(bf16[16,72,432]{2,1,0:T(8,128)(2,1)} %shard_map.64), calls=%async_computation | async-start | bytes 2359296 | tf_op jit(solution)/shard_map/all_to_all | solution.py:79
  30.5 0.0 copy-done.2
  30.5 0.6 fusion.7
  31.1 0.0 copy-done
  31.1 0.0 copy-done.1
  31.1 0.0 copy-done.3
  31.1 0.2 fusion
  31.4 4.4 %collective-permute-start.1 = (bf16[2,72,128]{2,1,0:T(8,128)(2,1)S(1)}, bf16[2,72,128]{2,1,0:T(8,128)(2,1)S(1)}, u32[]{:S(2)}, u32[]{:S(2)}) collective-permute-start(bf16[2,72,128]{2,1,0:T(8,128)(2,1)S(1)} %fusion), channel_id=1, source_target_pairs={{0,0},{1,8},{2,32},{3,40},{4,4},{5,12},{6,36},{7,44},{8,1},{9,9},{... | collective-permute-start | bytes 110600 | tf_op jit(solution)/shard_map/ppermute | solution.py:74
  35.8 4.0 %collective-permute-start.2 = (bf16[2,72,128]{2,1,0:T(8,128)(2,1)S(1)}, bf16[2,72,128]{2,1,0:T(8,128)(2,1)S(1)}, u32[]{:S(2)}, u32[]{:S(2)}) collective-permute-start(bf16[2,72,128]{2,1,0:T(8,128)(2,1)S(1)} %fusion), channel_id=1, source_target_pairs={{0,32},{1,40},{2,0},{3,8},{4,36},{5,44},{6,4},{7,12},{8,33},{9,41}... | collective-permute-start | bytes 110600 | tf_op jit(solution)/shard_map/ppermute | solution.py:75
  39.8 0.6 fusion.9
  46.2 0.1 collective-permute-done.1
  46.3 0.0 collective-permute-done.2
  46.4 1.2 %all-to-all-done = bf16[16,72,432]{2,1,0:T(8,128)(2,1)S(1)} async-done(((bf16[16,72,432]{2,1,0:T(8,128)(2,1)}), bf16[16,72,432]{2,1,0:T(8,128)(2,1)S(1)}, u32[]{:S(2)}, u32[]{:S(2)}) %all-to-all-start) | async-done | bytes 995360 | tf_op jit(solution)/shard_map/all_to_all | solution.py:79
  47.5 0.1 constant_dynamic-slice_fusion.2
  47.6 0.8 broadcast_in_dim.5
  48.4 13.9 %all-to-all-start.2 = ((bf16[6,2,2,72,128]{4,3,2,1,0:T(8,128)(2,1)}), bf16[6,2,2,72,128]{4,3,2,1,0:T(8,128)(2,1)S(1)}, u32[]{:S(2)}, u32[]{:S(2)}) async-start(bf16[6,2,2,72,128]{4,3,2,1,0:T(8,128)(2,1)} %broadcast_in_dim.5), calls=%async_computation.2 | async-start | bytes 884736 | tf_op jit(solution)/shard_map/all_to_all | solution.py:32
  62.3 2.2 %collective-permute-start.3 = (bf16[288,432]{1,0:T(8,128)(2,1)S(1)}, bf16[288,432]{1,0:T(8,128)(2,1)S(1)}, u32[]{:S(2)}, u32[]{:S(2)}) collective-permute-start(bf16[288,432]{1,0:T(8,128)(2,1)S(1)} %bitcast.42), channel_id=1, source_target_pairs={{0,4},{4,0},{1,5},{5,1},{2,6},{6,2},{3,7},{7,3},{8,12},{12,8},{9,1... | collective-permute-start | bytes 746504 | tf_op jit(solution)/shard_map/ppermute | solution.py:91
  64.5 9.9 %collective-permute-done.3 = bf16[288,432]{1,0:T(8,128)(2,1)S(1)} collective-permute-done((bf16[288,432]{1,0:T(8,128)(2,1)S(1)}, bf16[288,432]{1,0:T(8,128)(2,1)S(1)}, u32[]{:S(2)}, u32[]{:S(2)}) %collective-permute-start.3) | collective-permute-done | bytes 248864 | tf_op jit(solution)/shard_map/ppermute | solution.py:91
  74.4 6.5 %all-to-all-done.2 = bf16[6,2,2,72,128]{4,3,2,1,0:T(8,128)(2,1)S(1)} async-done(((bf16[6,2,2,72,128]{4,3,2,1,0:T(8,128)(2,1)}), bf16[6,2,2,72,128]{4,3,2,1,0:T(8,128)(2,1)S(1)}, u32[]{:S(2)}, u32[]{:S(2)}) %all-to-all-start.2) | async-done | bytes 442400 | tf_op jit(solution)/shard_map/all_to_all | solution.py:32
  80.9 3.9 %collective-permute-start.4 = (bf16[6,2,2,72,128]{4,3,2,1,0:T(8,128)(2,1)S(1)}, bf16[6,2,2,72,128]{4,3,2,1,0:T(8,128)(2,1)S(1)}, u32[]{:S(2)}, u32[]{:S(2)}) collective-permute-start(bf16[6,2,2,72,128]{4,3,2,1,0:T(8,128)(2,1)S(1)} %all-to-all-done.2), channel_id=1, source_target_pairs={{0,8},{8,0},{1,9},{9,1},{2,10},{10,2},{3,11},{11,3},{4,12},{12,4},... | collective-permute-start | bytes 1327112 | tf_op jit(solution)/shard_map/ppermute | solution.py:102
  84.8 0.6 fusion.8
  86.7 0.7 conditional.1
  86.7 0.7 copy.19
  87.4 1.3 %bitcast_select_fusion = (bf16[288,432]{1,0:T(8,128)(2,1)S(1)}, bf16[1,288,432]{2,1,0:T(8,128)(2,1)S(1)}) fusion(bf16[288,432]{1,0:T(8,128)(2,1)S(1)} %collective-permute-done.3, bf16[4,1,72,432]{3,2,1,0:T(8,128)(2,1)S(1)} %get-tuple-element.20, pred[]{:T(512)} %bitcast, bf16[288,432]{1,0:T(8,128)(2,1)} %get-tuple-element.35, pred[]{:T(512)} %bitcast.12, ...), kind=kLoop, calls=%fused_computation.12 | loop fusion | flops 373248 | bytes 1492995 | tf_op jit(solution)/shard_map/jit(_where)/select_n | solution.py:98
  88.7 0.0 collective-permute-done.4
  88.7 0.1 select_bitcast_fusion.1
  88.8 0.1 maximum_bitcast_fusion
  88.9 0.9 copy.12
  89.8 0.3 reshape.41
  90.1 0.5 convolution_convert_fusion
  90.6 0.1 convert_element_type.34
  90.7 0.1 copy.13
  90.8 0.0 copy-start.4
  90.8 16.1 %all_to_all.20 = bf16[16,2,72,128]{3,2,1,0:T(8,128)(2,1)S(1)} all-to-all(bf16[16,2,72,128]{3,2,1,0:T(8,128)(2,1)S(1)} %bitcast.40), channel_id=1, replica_groups=mesh['za'=6,'zb'=2,'ya'=2,'yb'=2,'core'=2,'yhi'=2,'x'=4] {'zb','yb','x'}, dimensions={0} | all-to-all | bytes 1179648 | tf_op jit(solution)/shard_map/all_to_all | solution.py:110
  107.0 0.1 convert_reduce_fusion
  107.1 0.0 copy-done.4
  107.1 0.7 add_convert_fusion
  (3 shorter events, 0.0 us)
Async XLA Ops:
  0.0 31.1 %copy-start = (bf16[2,1024,128]{2,1,0:T(8,128)(2,1)S(1)}, bf16[2,1024,128]{2,1,0:T(8,128)(2,1)}, u32[]{:S(2)}) copy-start(bf16[2,1024,128]{2,1,0:T(8,128)(2,1)} %param.9) | copy-start | bytes 1572868
  1.6 20.3 %all-to-all-start.1 = ((bf16[8,2,72,128]{3,2,1,0:T(8,128)(2,1)}), bf16[8,2,72,128]{3,2,1,0:T(8,128)(2,1)S(1)}, u32[]{:S(2)}, u32[]{:S(2)}) async-start(bf16[8,2,72,128]{3,2,1,0:T(8,128)(2,1)} %broadcast_in_dim.4), calls=%async_computation.1 | async-start | bytes 589824 | tf_op jit(solution)/shard_map/all_to_all | solution.py:32
  14.7 15.8 %copy-start.2 = (s32[2]{0:T(128)S(1)}, s32[2]{0:T(128)}, u32[]{:S(2)}) copy-start(s32[2]{0:T(128)} %param.11) | copy-start | bytes 28
  14.7 16.4 %copy-start.1 = (bf16[2,72,128]{2,1,0:T(8,128)(2,1)S(1)}, bf16[2,72,128]{2,1,0:T(8,128)(2,1)}, u32[]{:S(2)}) copy-start(bf16[2,72,128]{2,1,0:T(8,128)(2,1)} %param.8) | copy-start | bytes 110596
  14.7 16.4 %copy-start.3 = (f32[2]{0:T(128)S(1)}, f32[2]{0:T(128)}, u32[]{:S(2)}) copy-start(f32[2]{0:T(128)} %param.12) | copy-start | bytes 28
  21.9 25.6 %all-to-all-start = ((bf16[16,72,432]{2,1,0:T(8,128)(2,1)}), bf16[16,72,432]{2,1,0:T(8,128)(2,1)S(1)}, u32[]{:S(2)}, u32[]{:S(2)}) async-start(bf16[16,72,432]{2,1,0:T(8,128)(2,1)} %shard_map.64), calls=%async_computation | async-start | bytes 2359296 | tf_op jit(solution)/shard_map/all_to_all | solution.py:79
  31.4 14.9 %collective-permute-start.1 = (bf16[2,72,128]{2,1,0:T(8,128)(2,1)S(1)}, bf16[2,72,128]{2,1,0:T(8,128)(2,1)S(1)}, u32[]{:S(2)}, u32[]{:S(2)}) collective-permute-start(bf16[2,72,128]{2,1,0:T(8,128)(2,1)S(1)} %fusion), channel_id=1, source_target_pairs={{0,0},{1,8},{2,32},{3,40},{4,4},{5,12},{6,36},{7,44},{8,1},{9,9},{... | collective-permute-start | bytes 110600 | tf_op jit(solution)/shard_map/ppermute | solution.py:74
  35.8 10.5 %collective-permute-start.2 = (bf16[2,72,128]{2,1,0:T(8,128)(2,1)S(1)}, bf16[2,72,128]{2,1,0:T(8,128)(2,1)S(1)}, u32[]{:S(2)}, u32[]{:S(2)}) collective-permute-start(bf16[2,72,128]{2,1,0:T(8,128)(2,1)S(1)} %fusion), channel_id=1, source_target_pairs={{0,32},{1,40},{2,0},{3,8},{4,36},{5,44},{6,4},{7,12},{8,33},{9,41}... | collective-permute-start | bytes 110600 | tf_op jit(solution)/shard_map/ppermute | solution.py:75
  48.4 32.5 %all-to-all-start.2 = ((bf16[6,2,2,72,128]{4,3,2,1,0:T(8,128)(2,1)}), bf16[6,2,2,72,128]{4,3,2,1,0:T(8,128)(2,1)S(1)}, u32[]{:S(2)}, u32[]{:S(2)}) async-start(bf16[6,2,2,72,128]{4,3,2,1,0:T(8,128)(2,1)} %broadcast_in_dim.5), calls=%async_computation.2 | async-start | bytes 884736 | tf_op jit(solution)/shard_map/all_to_all | solution.py:32
  62.3 12.1 %collective-permute-start.3 = (bf16[288,432]{1,0:T(8,128)(2,1)S(1)}, bf16[288,432]{1,0:T(8,128)(2,1)S(1)}, u32[]{:S(2)}, u32[]{:S(2)}) collective-permute-start(bf16[288,432]{1,0:T(8,128)(2,1)S(1)} %bitcast.42), channel_id=1, source_target_pairs={{0,4},{4,0},{1,5},{5,1},{2,6},{6,2},{3,7},{7,3},{8,12},{12,8},{9,1... | collective-permute-start | bytes 746504 | tf_op jit(solution)/shard_map/ppermute | solution.py:91
  80.9 7.8 %collective-permute-start.4 = (bf16[6,2,2,72,128]{4,3,2,1,0:T(8,128)(2,1)S(1)}, bf16[6,2,2,72,128]{4,3,2,1,0:T(8,128)(2,1)S(1)}, u32[]{:S(2)}, u32[]{:S(2)}) collective-permute-start(bf16[6,2,2,72,128]{4,3,2,1,0:T(8,128)(2,1)S(1)} %all-to-all-done.2), channel_id=1, source_target_pairs={{0,8},{8,0},{1,9},{9,1},{2,10},{10,2},{3,11},{11,3},{4,12},{12,4},... | collective-permute-start | bytes 1327112 | tf_op jit(solution)/shard_map/ppermute | solution.py:102
  90.8 16.2 %copy-start.4 = (f32[2]{0:T(128)S(1)}, f32[2]{0:T(128)}, u32[]{:S(2)}) copy-start(f32[2]{0:T(128)} %param.13) | copy-start | bytes 28

commit v6 on v4

--- a/solution.py
+++ b/solution.py
@@ -87,12 +87,16 @@
     mine = [of_owner(owner_table[l]) for l in range(LAYERS)]
     one_half = owner_half[0] == owner_half[1]
     first = of_owner(jnp.where(here[0], owner_table[0], owner_table[1]))
-    first, piece = lax.optimization_barrier((first, piece))
     first = lax.ppermute(first, "yhi", FLIP)
     second = lax.cond(one_half, lambda part: lax.ppermute(part, "yhi", FLIP), lambda part: part, mine[1])
 
-    along = copies(piece, "za", BLOCKS)
-    along, first = lax.optimization_barrier((along, first))
+    za = lax.axis_index("za")
+    along = jnp.zeros((BLOCKS,) + piece.shape, piece.dtype)
+    for step in range(BLOCKS):
+        ahead = [((at + step) % BLOCKS, at) for at in range(BLOCKS)]
+        block = lax.ppermute(piece, "za", ahead) if step else piece
+        along = lax.dynamic_update_index_in_dim(along, block, (za + step) % BLOCKS, 0)
+    along, first, second = lax.optimization_barrier((along, first, second))
     factor = jnp.stack(
         [
             jnp.where(here[0], mine[0], first),

time: 138 us -> 132 us (0.957)
  waiting for transfers between devices: 39.3 us -> 15.7 us
  starting transfers between devices: 47.4 us -> 70.4 us
  blocking collectives: 27.5 us -> 23.6 us
    ppermute x1 -> x5, starting transfers between devices: 2.19 us -> 29.9 us  [body(): block = lax.ppermute(piece, 'za', ahead) if step else piece]
    all_to_all x2 -> x1, starting transfers between devices: 24 us -> 10.1 us  [copies(): lax.all_to_all(jnp.broadcast_to(value[None], (count,) + value.shape), axi...]
    ppermute x1 -> x5, waiting for transfers between devices: 12.5 us -> 3.41 us  [body(): block = lax.ppermute(piece, 'za', ahead) if step else piece]
    ppermute x1, starting transfers between devices: 3.9 us -> 11.1 us  [body(): chunk = ordered(along, lax.ppermute(along, 'core', FLIP), 'core')]
    all_to_all x2 -> x1, waiting for transfers between devices: 13.7 us -> 7.19 us  [copies(): lax.all_to_all(jnp.broadcast_to(value[None], (count,) + value.shape), axi...]
    ppermute x1, waiting for transfers between devices: 9.87 us -> 5.08 us  [body(): first = lax.ppermute(first, 'yhi', FLIP)]
    all_to_all x1, blocking collectives: 27.5 us -> 23.6 us  [body(): act = jnp.sum(lax.all_to_all(partial, CHUNK, 0, 0), axis=0)]
    ppermute x1, starting transfers between devices: 1.92 us -> 4.44 us  [body(): near = lax.ppermute(right, AXES, spread_pairs(0))]
  transfers between devices with their start and end apart: 8 -> 11, of which waited for: 7 -> 3; matrix products, arithmetic and copies ran while one was open for 3% -> 4% of each run, Pallas kernels for 2% -> 2%
where the time goes in v6:
time: 132 us; the launch traced here: 131 us
  starting transfers between devices  70.4 us (53%)
  blocking collectives  23.6 us (18%)
  waiting for transfers between devices  15.7 us (12%)
  between operations  7.07 us (5%)
  local copies, waits for them, and re-layouts  6.75 us (5%)
  other arithmetic  3.17 us (2%)
  Pallas kernels  3.02 us (2%)
  matrix products  1.75 us (1%)
    ppermute x5, starting transfers between devices, body(): block = lax.ppermute(piece, 'za', ahead) if step else piece  29.9 us
    all_to_all x1, blocking collectives, body(): act = jnp.sum(lax.all_to_all(partial, CHUNK, 0, 0), axis=0)  23.6 us
    ppermute x1, starting transfers between devices, body(): chunk = ordered(along, lax.ppermute(along, 'core', FLIP), 'core')  11.1 us
    all_to_all x1, starting transfers between devices, copies(): lax.all_to_all(jnp.broadcast_to(value[None], (count,) + value.shape), axi...  10.1 us
    all_to_all x1, starting transfers between devices, body(): lax.all_to_all(factor, CHUNK, 0, 0).reshape(N_ROWS, NX, rows, width)  8.58 us
    all_to_all x1, waiting for transfers between devices, copies(): lax.all_to_all(jnp.broadcast_to(value[None], (count,) + value.shape), axi...  7.19 us
    ppermute x1, waiting for transfers between devices, body(): first = lax.ppermute(first, 'yhi', FLIP)  5.08 us
    ppermute x1, starting transfers between devices, body(): near = lax.ppermute(right, AXES, spread_pairs(0))  4.44 us
  transfers between devices with their start and end apart: 11, of which 3 were waited for; matrix products, arithmetic and copies ran while one was open for 4% of the time, Pallas kernels for 2%

profile of v6, /device:TPU:1, one launch (start us, length us, event | category | flops | bytes accessed | tf_op | source)
XLA Modules:
  0.0 131.4 jit_solution(4207065514441861731)
XLA Ops:
  0.0 0.0 copy-start
  0.0 1.6 %broadcast_in_dim.31 = bf16[8,2,72,128]{3,2,1,0:T(8,128)(2,1)} broadcast(bf16[2,72,128]{2,1,0:T(8,128)(2,1)} %param.8), dimensions={1,2,3} | broadcast | bytes 331776 | tf_op jit(solution)/shard_map/broadcast_in_dim | solution.py:32
  1.6 10.1 %all-to-all-start.1 = ((bf16[8,2,72,128]{3,2,1,0:T(8,128)(2,1)}), bf16[8,2,72,128]{3,2,1,0:T(8,128)(2,1)S(1)}, u32[]{:S(2)}, u32[]{:S(2)}) async-start(bf16[8,2,72,128]{3,2,1,0:T(8,128)(2,1)} %broadcast_in_dim.31), calls=%async_computation.1 | async-start | bytes 589824 | tf_op jit(solution)/shard_map/all_to_all | solution.py:32
  11.7 3.0 %shard_map.64 = bf16[16,72,432]{2,1,0:T(8,128)(2,1)} custom-call(bf16[1,72,6912]{2,1,0:T(8,128)(2,1)} %factor_ref.1), custom_call_target="tpu_custom_call" | custom-call | bytes 1990656 | tf_op jit(solution)/shard_map/pallas_call | solution.py:53
  14.7 7.2 %all-to-all-done.1 = bf16[8,2,72,128]{3,2,1,0:T(8,128)(2,1)S(1)} async-done(((bf16[8,2,72,128]{3,2,1,0:T(8,128)(2,1)}), bf16[8,2,72,128]{3,2,1,0:T(8,128)(2,1)S(1)}, u32[]{:S(2)}, u32[]{:S(2)}) %all-to-all-start.1) | async-done | bytes 294944 | tf_op jit(solution)/shard_map/all_to_all | solution.py:32
  21.9 8.6 %all-to-all-start = ((bf16[16,72,432]{2,1,0:T(8,128)(2,1)}), bf16[16,72,432]{2,1,0:T(8,128)(2,1)S(1)}, u32[]{:S(2)}, u32[]{:S(2)}) async-start(bf16[16,72,432]{2,1,0:T(8,128)(2,1)} %shard_map.64), calls=%async_computation | async-start | bytes 2359296 | tf_op jit(solution)/shard_map/all_to_all | solution.py:79
  30.5 0.0 copy-done.2
  30.5 0.6 fusion.10
  31.1 0.6 fusion.8
  31.7 0.0 copy-done
  31.7 0.0 copy-done.1
  31.7 0.2 fusion
  32.0 4.4 %collective-permute-start.1 = (bf16[2,72,128]{2,1,0:T(8,128)(2,1)S(1)}, bf16[2,72,128]{2,1,0:T(8,128)(2,1)S(1)}, u32[]{:S(2)}, u32[]{:S(2)}) collective-permute-start(bf16[2,72,128]{2,1,0:T(8,128)(2,1)S(1)} %fusion), channel_id=1, source_target_pairs={{0,0},{1,8},{2,32},{3,40},{4,4},{5,12},{6,36},{7,44},{8,1},{9,9},{... | collective-permute-start | bytes 110600 | tf_op jit(solution)/shard_map/ppermute | solution.py:74
  36.4 4.0 %collective-permute-start.2 = (bf16[2,72,128]{2,1,0:T(8,128)(2,1)S(1)}, bf16[2,72,128]{2,1,0:T(8,128)(2,1)S(1)}, u32[]{:S(2)}, u32[]{:S(2)}) collective-permute-start(bf16[2,72,128]{2,1,0:T(8,128)(2,1)S(1)} %fusion), channel_id=1, source_target_pairs={{0,32},{1,40},{2,0},{3,8},{4,36},{5,44},{6,4},{7,12},{8,33},{9,41}... | collective-permute-start | bytes 110600 | tf_op jit(solution)/shard_map/ppermute | solution.py:75
  40.4 0.7 fusion.9
  47.9 0.0 collective-permute-done.1
  47.9 0.0 collective-permute-done.2
  47.9 13.4 %collective-permute-start.3 = (bf16[2,2,72,128]{3,2,1,0:T(8,128)(2,1)S(1)}, bf16[2,2,72,128]{3,2,1,0:T(8,128)(2,1)S(1)}, u32[]{:S(2)}, u32[]{:S(2)}) collective-permute-start(bf16[2,2,72,128]{3,2,1,0:T(8,128)(2,1)S(1)} %pad_maximum_fusion), channel_id=1, source_target_pairs={{128,0},{256,128},{384,256},{512,384},{640,512},{0,640},{129,1},{2... | collective-permute-start | bytes 221192 | tf_op jit(solution)/shard_map/ppermute | solution.py:97
  61.3 3.4 %collective-permute-start.4 = (bf16[2,2,72,128]{3,2,1,0:T(8,128)(2,1)S(1)}, bf16[2,2,72,128]{3,2,1,0:T(8,128)(2,1)S(1)}, u32[]{:S(2)}, u32[]{:S(2)}) collective-permute-start(bf16[2,2,72,128]{3,2,1,0:T(8,128)(2,1)S(1)} %pad_maximum_fusion), channel_id=1, source_target_pairs={{256,0},{384,128},{512,256},{640,384},{0,512},{128,640},{257,1},{3... | collective-permute-start | bytes 221192 | tf_op jit(solution)/shard_map/ppermute | solution.py:97
  64.7 1.9 %collective-permute-start.5 = (bf16[2,2,72,128]{3,2,1,0:T(8,128)(2,1)S(1)}, bf16[2,2,72,128]{3,2,1,0:T(8,128)(2,1)S(1)}, u32[]{:S(2)}, u32[]{:S(2)}) collective-permute-start(bf16[2,2,72,128]{3,2,1,0:T(8,128)(2,1)S(1)} %pad_maximum_fusion), channel_id=1, source_target_pairs={{384,0},{512,128},{640,256},{0,384},{128,512},{256,640},{385,1},{5... | collective-permute-start | bytes 221192 | tf_op jit(solution)/shard_map/ppermute | solution.py:97
  66.6 7.0 %collective-permute-start.6 = (bf16[2,2,72,128]{3,2,1,0:T(8,128)(2,1)S(1)}, bf16[2,2,72,128]{3,2,1,0:T(8,128)(2,1)S(1)}, u32[]{:S(2)}, u32[]{:S(2)}) collective-permute-start(bf16[2,2,72,128]{3,2,1,0:T(8,128)(2,1)S(1)} %pad_maximum_fusion), channel_id=1, source_target_pairs={{512,0},{640,128},{0,256},{128,384},{256,512},{384,640},{513,1},{6... | collective-permute-start | bytes 221192 | tf_op jit(solution)/shard_map/ppermute | solution.py:97
  73.6 4.3 %collective-permute-start.7 = (bf16[2,2,72,128]{3,2,1,0:T(8,128)(2,1)S(1)}, bf16[2,2,72,128]{3,2,1,0:T(8,128)(2,1)S(1)}, u32[]{:S(2)}, u32[]{:S(2)}) collective-permute-start(bf16[2,2,72,128]{3,2,1,0:T(8,128)(2,1)S(1)} %pad_maximum_fusion), channel_id=1, source_target_pairs={{640,0},{0,128},{128,256},{256,384},{384,512},{512,640},{641,1},{1... | collective-permute-start | bytes 221192 | tf_op jit(solution)/shard_map/ppermute | solution.py:97
  77.9 0.1 broadcast_in_dim.30
  78.0 0.0 collective-permute-done.3
  78.0 0.0 collective-permute-done.4
  78.1 0.0 collective-permute-done.5
  78.1 0.0 all-to-all-done
  78.1 0.1 constant_dynamic-slice_fusion.2
  78.2 2.2 %collective-permute-start.8 = (bf16[288,432]{1,0:T(8,128)(2,1)S(1)}, bf16[288,432]{1,0:T(8,128)(2,1)S(1)}, u32[]{:S(2)}, u32[]{:S(2)}) collective-permute-start(bf16[288,432]{1,0:T(8,128)(2,1)S(1)} %bitcast.54), channel_id=1, source_target_pairs={{0,4},{4,0},{1,5},{5,1},{2,6},{6,2},{3,7},{7,3},{8,12},{12,8},{9,1... | collective-permute-start | bytes 746504 | tf_op jit(solution)/shard_map/ppermute | solution.py:90
  80.4 0.0 collective-permute-done.6
  80.4 3.4 %collective-permute-done.7 = bf16[2,2,72,128]{3,2,1,0:T(8,128)(2,1)S(1)} collective-permute-done((bf16[2,2,72,128]{3,2,1,0:T(8,128)(2,1)S(1)}, bf16[2,2,72,128]{3,2,1,0:T(8,128)(2,1)S(1)}, u32[]{:S(2)}, u32[]{:S(2)}) %collective-permute-start.7) | collective-permute-done | bytes 73760 | tf_op jit(solution)/shard_map/ppermute | solution.py:97
  83.9 0.7 conditional.1
  83.9 0.7 copy.24
  84.6 5.1 %collective-permute-done.8 = bf16[288,432]{1,0:T(8,128)(2,1)S(1)} collective-permute-done((bf16[288,432]{1,0:T(8,128)(2,1)S(1)}, bf16[288,432]{1,0:T(8,128)(2,1)S(1)}, u32[]{:S(2)}, u32[]{:S(2)}) %collective-permute-start.8) | collective-permute-done | bytes 248864 | tf_op jit(solution)/shard_map/ppermute | solution.py:90
  89.7 11.1 %collective-permute-start.9 = (bf16[6,2,2,72,128]{4,3,2,1,0:T(8,128)(2,1)S(1)}, bf16[6,2,2,72,128]{4,3,2,1,0:T(8,128)(2,1)S(1)}, u32[]{:S(2)}, u32[]{:S(2)}) collective-permute-start(bf16[6,2,2,72,128]{4,3,2,1,0:T(8,128)(2,1)S(1)} %bitcast_dynamic-update-slice_fusion), channel_id=1, source_target_pairs={{0,8},{8,0},{1,9},{9,1},{2,10},{10,2},{3,11},{11,3},{4,12},{12,4},... | collective-permute-start | bytes 1327112 | tf_op jit(solution)/shard_map/ppermute | solution.py:106
  100.8 2.2 %bitcast_select_fusion = (bf16[288,432]{1,0:T(8,128)(2,1)}, bf16[1,288,432]{2,1,0:T(8,128)(2,1)}) fusion(bf16[288,432]{1,0:T(8,128)(2,1)S(1)} %collective-permute-done.8, bf16[4,1,72,432]{3,2,1,0:T(8,128)(2,1)S(1)} %get-tuple-element.18, pred[]{:T(512)} %bitcast, bf16[288,432]{1,0:T(8,128)(2,1)} %get-tuple-element.33, pred[]{:T(512)} %bitcast.15, ...), kind=kLoop, calls=%fused_computation.11 | loop fusion | flops 373248 | bytes 1492995 | tf_op jit(solution)/shard_map/jit(_where)/select_n | solution.py:102
  103.0 0.0 collective-permute-done.9
  103.1 0.1 select_bitcast_fusion.1
  103.1 0.1 maximum_bitcast_fusion
  103.2 0.9 copy.11
  104.1 0.3 reshape.42
  104.5 1.5 %fusion.1 = f32[2,288,512]{2,1,0:T(8,128)S(1)} fusion(bf16[2,432,512]{2,1,0:T(8,128)(2,1)S(1)} %reshape.42, bf16[1,288,432]{2,1,0:T(8,128)(2,1)} %get-tuple-element.24, bf16[1,288,432]{2,1,0:T(8,128)(2,1)} %bitcast.53), kind=kOutput, calls=%fused_computation.3 | convolution fusion | flops 255052800 | bytes 2562048 | tf_op jit(solution)/shard_map/dot_general | solution.py:109
  106.0 0.4 reshape.43
  106.4 0.1 copy.12
  106.5 23.6 %all_to_all.15 = f32[16,2,72,128]{3,2,1,0:T(8,128)S(1)} all-to-all(f32[16,2,72,128]{3,2,1,0:T(8,128)S(1)} %bitcast.49), channel_id=1, replica_groups=mesh['za'=6,'zb'=2,'ya'=2,'yb'=2,'core'=2,'yhi'=2,'x'=4] {'zb','yb','x'}, dimensions={0} | all-to-all | bytes 2359296 | tf_op jit(solution)/shard_map/all_to_all | solution.py:114
  130.1 0.1 reduce_sum.9
  130.1 0.6 copy-done.4
  130.7 0.7 add_convert_fusion
  (14 shorter events, 0.1 us)
Async XLA Ops:
  0.0 31.7 %copy-start = (bf16[2,1024,128]{2,1,0:T(8,128)(2,1)S(1)}, bf16[2,1024,128]{2,1,0:T(8,128)(2,1)}, u32[]{:S(2)}) copy-start(bf16[2,1024,128]{2,1,0:T(8,128)(2,1)} %param.9) | copy-start | bytes 1572868
  1.6 20.3 %all-to-all-start.1 = ((bf16[8,2,72,128]{3,2,1,0:T(8,128)(2,1)}), bf16[8,2,72,128]{3,2,1,0:T(8,128)(2,1)S(1)}, u32[]{:S(2)}, u32[]{:S(2)}) async-start(bf16[8,2,72,128]{3,2,1,0:T(8,128)(2,1)} %broadcast_in_dim.31), calls=%async_computation.1 | async-start | bytes 589824 | tf_op jit(solution)/shard_map/all_to_all | solution.py:32
  14.7 15.8 %copy-start.2 = (s32[2]{0:T(128)S(1)}, s32[2]{0:T(128)}, u32[]{:S(2)}) copy-start(s32[2]{0:T(128)} %param.11) | copy-start | bytes 28
  14.7 17.0 %copy-start.1 = (bf16[2,72,128]{2,1,0:T(8,128)(2,1)S(1)}, bf16[2,72,128]{2,1,0:T(8,128)(2,1)}, u32[]{:S(2)}) copy-start(bf16[2,72,128]{2,1,0:T(8,128)(2,1)} %param.8) | copy-start | bytes 110596
  14.7 17.0 %copy-start.3 = (f32[2]{0:T(128)S(1)}, f32[2]{0:T(128)}, u32[]{:S(2)}) copy-start(f32[2]{0:T(128)} %param.12) | copy-start | bytes 28
  21.9 56.2 %all-to-all-start = ((bf16[16,72,432]{2,1,0:T(8,128)(2,1)}), bf16[16,72,432]{2,1,0:T(8,128)(2,1)S(1)}, u32[]{:S(2)}, u32[]{:S(2)}) async-start(bf16[16,72,432]{2,1,0:T(8,128)(2,1)} %shard_map.64), calls=%async_computation | async-start | bytes 2359296 | tf_op jit(solution)/shard_map/all_to_all | solution.py:79
  32.0 15.9 %collective-permute-start.1 = (bf16[2,72,128]{2,1,0:T(8,128)(2,1)S(1)}, bf16[2,72,128]{2,1,0:T(8,128)(2,1)S(1)}, u32[]{:S(2)}, u32[]{:S(2)}) collective-permute-start(bf16[2,72,128]{2,1,0:T(8,128)(2,1)S(1)} %fusion), channel_id=1, source_target_pairs={{0,0},{1,8},{2,32},{3,40},{4,4},{5,12},{6,36},{7,44},{8,1},{9,9},{... | collective-permute-start | bytes 110600 | tf_op jit(solution)/shard_map/ppermute | solution.py:74
  36.4 11.5 %collective-permute-start.2 = (bf16[2,72,128]{2,1,0:T(8,128)(2,1)S(1)}, bf16[2,72,128]{2,1,0:T(8,128)(2,1)S(1)}, u32[]{:S(2)}, u32[]{:S(2)}) collective-permute-start(bf16[2,72,128]{2,1,0:T(8,128)(2,1)S(1)} %fusion), channel_id=1, source_target_pairs={{0,32},{1,40},{2,0},{3,8},{4,36},{5,44},{6,4},{7,12},{8,33},{9,41}... | collective-permute-start | bytes 110600 | tf_op jit(solution)/shard_map/ppermute | solution.py:75
  47.9 30.1 %collective-permute-start.3 = (bf16[2,2,72,128]{3,2,1,0:T(8,128)(2,1)S(1)}, bf16[2,2,72,128]{3,2,1,0:T(8,128)(2,1)S(1)}, u32[]{:S(2)}, u32[]{:S(2)}) collective-permute-start(bf16[2,2,72,128]{3,2,1,0:T(8,128)(2,1)S(1)} %pad_maximum_fusion), channel_id=1, source_target_pairs={{128,0},{256,128},{384,256},{512,384},{640,512},{0,640},{129,1},{2... | collective-permute-start | bytes 221192 | tf_op jit(solution)/shard_map/ppermute | solution.py:97
  61.3 16.7 %collective-permute-start.4 = (bf16[2,2,72,128]{3,2,1,0:T(8,128)(2,1)S(1)}, bf16[2,2,72,128]{3,2,1,0:T(8,128)(2,1)S(1)}, u32[]{:S(2)}, u32[]{:S(2)}) collective-permute-start(bf16[2,2,72,128]{3,2,1,0:T(8,128)(2,1)S(1)} %pad_maximum_fusion), channel_id=1, source_target_pairs={{256,0},{384,128},{512,256},{640,384},{0,512},{128,640},{257,1},{3... | collective-permute-start | bytes 221192 | tf_op jit(solution)/shard_map/ppermute | solution.py:97
  64.7 13.4 %collective-permute-start.5 = (bf16[2,2,72,128]{3,2,1,0:T(8,128)(2,1)S(1)}, bf16[2,2,72,128]{3,2,1,0:T(8,128)(2,1)S(1)}, u32[]{:S(2)}, u32[]{:S(2)}) collective-permute-start(bf16[2,2,72,128]{3,2,1,0:T(8,128)(2,1)S(1)} %pad_maximum_fusion), channel_id=1, source_target_pairs={{384,0},{512,128},{640,256},{0,384},{128,512},{256,640},{385,1},{5... | collective-permute-start | bytes 221192 | tf_op jit(solution)/shard_map/ppermute | solution.py:97
  66.6 13.8 %collective-permute-start.6 = (bf16[2,2,72,128]{3,2,1,0:T(8,128)(2,1)S(1)}, bf16[2,2,72,128]{3,2,1,0:T(8,128)(2,1)S(1)}, u32[]{:S(2)}, u32[]{:S(2)}) collective-permute-start(bf16[2,2,72,128]{3,2,1,0:T(8,128)(2,1)S(1)} %pad_maximum_fusion), channel_id=1, source_target_pairs={{512,0},{640,128},{0,256},{128,384},{256,512},{384,640},{513,1},{6... | collective-permute-start | bytes 221192 | tf_op jit(solution)/shard_map/ppermute | solution.py:97
  73.6 10.2 %collective-permute-start.7 = (bf16[2,2,72,128]{3,2,1,0:T(8,128)(2,1)S(1)}, bf16[2,2,72,128]{3,2,1,0:T(8,128)(2,1)S(1)}, u32[]{:S(2)}, u32[]{:S(2)}) collective-permute-start(bf16[2,2,72,128]{3,2,1,0:T(8,128)(2,1)S(1)} %pad_maximum_fusion), channel_id=1, source_target_pairs={{640,0},{0,128},{128,256},{256,384},{384,512},{512,640},{641,1},{1... | collective-permute-start | bytes 221192 | tf_op jit(solution)/shard_map/ppermute | solution.py:97
  78.2 11.5 %collective-permute-start.8 = (bf16[288,432]{1,0:T(8,128)(2,1)S(1)}, bf16[288,432]{1,0:T(8,128)(2,1)S(1)}, u32[]{:S(2)}, u32[]{:S(2)}) collective-permute-start(bf16[288,432]{1,0:T(8,128)(2,1)S(1)} %bitcast.54), channel_id=1, source_target_pairs={{0,4},{4,0},{1,5},{5,1},{2,6},{6,2},{3,7},{7,3},{8,12},{12,8},{9,1... | collective-permute-start | bytes 746504 | tf_op jit(solution)/shard_map/ppermute | solution.py:90
  89.7 13.4 %collective-permute-start.9 = (bf16[6,2,2,72,128]{4,3,2,1,0:T(8,128)(2,1)S(1)}, bf16[6,2,2,72,128]{4,3,2,1,0:T(8,128)(2,1)S(1)}, u32[]{:S(2)}, u32[]{:S(2)}) collective-permute-start(bf16[6,2,2,72,128]{4,3,2,1,0:T(8,128)(2,1)S(1)} %bitcast_dynamic-update-slice_fusion), channel_id=1, source_target_pairs={{0,8},{8,0},{1,9},{9,1},{2,10},{10,2},{3,11},{11,3},{4,12},{12,4},... | collective-permute-start | bytes 1327112 | tf_op jit(solution)/shard_map/ppermute | solution.py:106
  130.1 0.7 copy-start.4

commit v7 on v4

--- a/solution.py
+++ b/solution.py
@@ -92,7 +92,7 @@
     second = lax.cond(one_half, lambda part: lax.ppermute(part, "yhi", FLIP), lambda part: part, mine[1])
 
     along = copies(piece, "za", BLOCKS)
-    along, first = lax.optimization_barrier((along, first))
+    along, first, second = lax.optimization_barrier((along, first, second))
     factor = jnp.stack(
         [
             jnp.where(here[0], mine[0], first),

time: 138 us -> 129 us (0.935)
  waiting for transfers between devices: 39.3 us -> 24.3 us
  starting transfers between devices: 47.4 us -> 55.4 us
  blocking collectives: 27.5 us -> 25.5 us
    ppermute x1, waiting for transfers between devices: 9.87 us -> 0.01 us  [body(): first = lax.ppermute(first, 'yhi', FLIP)]
    all_to_all x2, waiting for transfers between devices: 13.7 us -> 7.19 us  [copies(): lax.all_to_all(jnp.broadcast_to(value[None], (count,) + value.shape), axi...]
    ppermute x1, starting transfers between devices: 2.19 us -> 7 us  [body(): lax.ppermute(part, 'yhi', FLIP)]
    ppermute x1, starting transfers between devices: 3.9 us -> 7.18 us  [body(): chunk = ordered(along, lax.ppermute(along, 'core', FLIP), 'core')]
    all_to_all x1, blocking collectives: 27.5 us -> 25.5 us  [body(): act = jnp.sum(lax.all_to_all(partial, CHUNK, 0, 0), axis=0)]
    ppermute x1, waiting for transfers between devices: 12.5 us -> 13.9 us  [body(): lax.ppermute(part, 'yhi', FLIP)]
  transfers between devices with their start and end apart: 8 -> 8, of which waited for: 7 -> 5; matrix products, arithmetic and copies ran while one was open for 3% -> 3% of each run, Pallas kernels for 2% -> 2%
where the time goes in v7:
time: 129 us; the launch traced here: 128 us
  starting transfers between devices  55.4 us (43%)
  blocking collectives  25.5 us (20%)
  waiting for transfers between devices  24.3 us (19%)
  local copies, waits for them, and re-layouts  7.48 us (6%)
  between operations  7.26 us (6%)
  other arithmetic  3.15 us (2%)
  Pallas kernels  3.02 us (2%)
  matrix products  1.87 us (1%)
    all_to_all x1, blocking collectives, body(): act = jnp.sum(lax.all_to_all(partial, CHUNK, 0, 0), axis=0)  25.5 us
    all_to_all x2, starting transfers between devices, copies(): lax.all_to_all(jnp.broadcast_to(value[None], (count,) + value.shape), axi...  24 us
    ppermute x1, waiting for transfers between devices, body(): lax.ppermute(part, 'yhi', FLIP)  13.9 us
    all_to_all x1, starting transfers between devices, body(): lax.all_to_all(factor, CHUNK, 0, 0).reshape(N_ROWS, NX, rows, width)  8.58 us
    all_to_all x2, waiting for transfers between devices, copies(): lax.all_to_all(jnp.broadcast_to(value[None], (count,) + value.shape), axi...  7.19 us
    ppermute x1, starting transfers between devices, body(): chunk = ordered(along, lax.ppermute(along, 'core', FLIP), 'core')  7.18 us
    ppermute x1, starting transfers between devices, body(): lax.ppermute(part, 'yhi', FLIP)  7 us
    ppermute x1, starting transfers between devices, body(): far = lax.ppermute(right, AXES, spread_pairs(1))  4.55 us
  transfers between devices with their start and end apart: 8, of which 5 were waited for; matrix products, arithmetic and copies ran while one was open for 3% of the time, Pallas kernels for 2%

profile of v7, /device:TPU:1, one launch (start us, length us, event | category | flops | bytes accessed | tf_op | source)
XLA Modules:
  0.0 128.1 jit_solution(12360065484450707318)
XLA Ops:
  0.0 0.0 copy-start
  0.0 1.6 %broadcast_in_dim.4 = bf16[8,2,72,128]{3,2,1,0:T(8,128)(2,1)} broadcast(bf16[2,72,128]{2,1,0:T(8,128)(2,1)} %param.8), dimensions={1,2,3} | broadcast | bytes 331776 | tf_op jit(solution)/shard_map/broadcast_in_dim | solution.py:32
  1.6 10.1 %all-to-all-start.1 = ((bf16[8,2,72,128]{3,2,1,0:T(8,128)(2,1)}), bf16[8,2,72,128]{3,2,1,0:T(8,128)(2,1)S(1)}, u32[]{:S(2)}, u32[]{:S(2)}) async-start(bf16[8,2,72,128]{3,2,1,0:T(8,128)(2,1)} %broadcast_in_dim.4), calls=%async_computation.1 | async-start | bytes 589824 | tf_op jit(solution)/shard_map/all_to_all | solution.py:32
  11.7 3.0 %shard_map.64 = bf16[16,72,432]{2,1,0:T(8,128)(2,1)} custom-call(bf16[1,72,6912]{2,1,0:T(8,128)(2,1)} %factor_ref.1), custom_call_target="tpu_custom_call" | custom-call | bytes 1990656 | tf_op jit(solution)/shard_map/pallas_call | solution.py:53
  14.7 0.0 copy-start.2
  14.7 0.0 copy-start.1
  14.7 0.0 copy-start.3
  14.7 7.2 %all-to-all-done.1 = bf16[8,2,72,128]{3,2,1,0:T(8,128)(2,1)S(1)} async-done(((bf16[8,2,72,128]{3,2,1,0:T(8,128)(2,1)}), bf16[8,2,72,128]{3,2,1,0:T(8,128)(2,1)S(1)}, u32[]{:S(2)}, u32[]{:S(2)}) %all-to-all-start.1) | async-done | bytes 294944 | tf_op jit(solution)/shard_map/all_to_all | solution.py:32
  21.9 8.6 %all-to-all-start = ((bf16[16,72,432]{2,1,0:T(8,128)(2,1)}), bf16[16,72,432]{2,1,0:T(8,128)(2,1)S(1)}, u32[]{:S(2)}, u32[]{:S(2)}) async-start(bf16[16,72,432]{2,1,0:T(8,128)(2,1)} %shard_map.64), calls=%async_computation | async-start | bytes 2359296 | tf_op jit(solution)/shard_map/all_to_all | solution.py:79
  30.5 0.0 copy-done.2
  30.5 0.6 fusion.8
  31.1 0.0 copy-done
  31.1 0.0 copy-done.1
  31.1 0.0 copy-done.3
  31.1 0.2 fusion
  31.4 4.5 %collective-permute-start.2 = (bf16[2,72,128]{2,1,0:T(8,128)(2,1)S(1)}, bf16[2,72,128]{2,1,0:T(8,128)(2,1)S(1)}, u32[]{:S(2)}, u32[]{:S(2)}) collective-permute-start(bf16[2,72,128]{2,1,0:T(8,128)(2,1)S(1)} %fusion), channel_id=1, source_target_pairs={{0,32},{1,40},{2,0},{3,8},{4,36},{5,44},{6,4},{7,12},{8,33},{9,41}... | collective-permute-start | bytes 110600 | tf_op jit(solution)/shard_map/ppermute | solution.py:75
  35.9 1.9 %collective-permute-start.1 = (bf16[2,72,128]{2,1,0:T(8,128)(2,1)S(1)}, bf16[2,72,128]{2,1,0:T(8,128)(2,1)S(1)}, u32[]{:S(2)}, u32[]{:S(2)}) collective-permute-start(bf16[2,72,128]{2,1,0:T(8,128)(2,1)S(1)} %fusion), channel_id=1, source_target_pairs={{0,0},{1,8},{2,32},{3,40},{4,4},{5,12},{6,36},{7,44},{8,1},{9,9},{... | collective-permute-start | bytes 110600 | tf_op jit(solution)/shard_map/ppermute | solution.py:74
  37.9 0.6 fusion.10
  44.2 1.7 %collective-permute-done.2 = bf16[2,72,128]{2,1,0:T(8,128)(2,1)S(1)} collective-permute-done((bf16[2,72,128]{2,1,0:T(8,128)(2,1)S(1)}, bf16[2,72,128]{2,1,0:T(8,128)(2,1)S(1)}, u32[]{:S(2)}, u32[]{:S(2)}) %collective-permute-start.2) | collective-permute-done | bytes 36896 | tf_op jit(solution)/shard_map/ppermute | solution.py:75
  46.0 0.1 collective-permute-done.1
  46.1 1.5 %all-to-all-done = bf16[16,72,432]{2,1,0:T(8,128)(2,1)S(1)} async-done(((bf16[16,72,432]{2,1,0:T(8,128)(2,1)}), bf16[16,72,432]{2,1,0:T(8,128)(2,1)S(1)}, u32[]{:S(2)}, u32[]{:S(2)}) %all-to-all-start) | async-done | bytes 995360 | tf_op jit(solution)/shard_map/all_to_all | solution.py:79
  47.5 0.1 constant_dynamic-slice_fusion.2
  47.6 0.8 broadcast_in_dim.5
  48.4 13.9 %all-to-all-start.2 = ((bf16[6,2,2,72,128]{4,3,2,1,0:T(8,128)(2,1)}), bf16[6,2,2,72,128]{4,3,2,1,0:T(8,128)(2,1)S(1)}, u32[]{:S(2)}, u32[]{:S(2)}) async-start(bf16[6,2,2,72,128]{4,3,2,1,0:T(8,128)(2,1)} %broadcast_in_dim.5), calls=%async_computation.2 | async-start | bytes 884736 | tf_op jit(solution)/shard_map/all_to_all | solution.py:32
  62.3 2.2 %collective-permute-start.3 = (bf16[288,432]{1,0:T(8,128)(2,1)S(1)}, bf16[288,432]{1,0:T(8,128)(2,1)S(1)}, u32[]{:S(2)}, u32[]{:S(2)}) collective-permute-start(bf16[288,432]{1,0:T(8,128)(2,1)S(1)} %bitcast.42), channel_id=1, source_target_pairs={{0,4},{4,0},{1,5},{5,1},{2,6},{6,2},{3,7},{7,3},{8,12},{12,8},{9,1... | collective-permute-start | bytes 746504 | tf_op jit(solution)/shard_map/ppermute | solution.py:91
  64.5 0.6 fusion.9
  66.4 20.9 %conditional.1 = (bf16[288,432]{1,0:T(8,128)(2,1)}) conditional(s32[]{:T(128)} %convert_element_type.17, bf16[288,432]{1,0:T(8,128)(2,1)S(1)} %bitcast.39, bf16[288,432]{1,0:T(8,128)(2,1)S(1)} %bitcast.40), branch_computations={%region_0.1_spmd, %region_1.2_spmd} | conditional | bytes 995376 | solution.py:92
  66.4 7.0 %collective-permute-start = (bf16[288,432]{1,0:T(8,128)(2,1)S(1)}, bf16[288,432]{1,0:T(8,128)(2,1)}, u32[]{:S(2)}, u32[]{:S(2)}) collective-permute-start(bf16[288,432]{1,0:T(8,128)(2,1)S(1)} %param.1), channel_id=1, source_target_pairs={{0,4},{4,0},{1,5},{5,1},{2,6},{6,2},{3,7},{7,3},{8,12},{12,8},{9,1... | collective-permute-start | bytes 746504 | tf_op jit(solution)/shard_map/cond/branch_1_fun/ppermute | solution.py:92
  73.4 13.9 %collective-permute-done = bf16[288,432]{1,0:T(8,128)(2,1)} collective-permute-done((bf16[288,432]{1,0:T(8,128)(2,1)S(1)}, bf16[288,432]{1,0:T(8,128)(2,1)}, u32[]{:S(2)}, u32[]{:S(2)}) %collective-permute-start) | collective-permute-done | bytes 248864 | tf_op jit(solution)/shard_map/cond/branch_1_fun/ppermute | solution.py:92
  87.3 0.0 collective-permute-done.3
  87.3 0.0 all-to-all-done.2
  87.3 7.2 %collective-permute-start.4 = (bf16[6,2,2,72,128]{4,3,2,1,0:T(8,128)(2,1)S(1)}, bf16[6,2,2,72,128]{4,3,2,1,0:T(8,128)(2,1)S(1)}, u32[]{:S(2)}, u32[]{:S(2)}) collective-permute-start(bf16[6,2,2,72,128]{4,3,2,1,0:T(8,128)(2,1)S(1)} %all-to-all-done.2), channel_id=1, source_target_pairs={{0,8},{8,0},{1,9},{9,1},{2,10},{10,2},{3,11},{11,3},{4,12},{12,4},... | collective-permute-start | bytes 1327112 | tf_op jit(solution)/shard_map/ppermute | solution.py:102
  94.5 2.2 %bitcast_select_fusion = (bf16[288,432]{1,0:T(8,128)(2,1)S(1)}, bf16[1,288,432]{2,1,0:T(8,128)(2,1)S(1)}) fusion(bf16[288,432]{1,0:T(8,128)(2,1)S(1)} %collective-permute-done.3, bf16[4,1,72,432]{3,2,1,0:T(8,128)(2,1)S(1)} %get-tuple-element.22, pred[]{:T(512)} %bitcast, bf16[288,432]{1,0:T(8,128)(2,1)} %get-tuple-element.37, pred[]{:T(512)} %bitcast.9, ...), kind=kLoop, calls=%fused_computation.11 | loop fusion | flops 373248 | bytes 1492995 | tf_op jit(solution)/shard_map/jit(_where)/select_n | solution.py:98
  96.7 0.0 collective-permute-done.4
  96.7 0.1 select_bitcast_fusion.1
  96.8 0.1 maximum_bitcast_fusion
  96.9 0.9 copy.12
  97.8 1.3 reshape.43
  99.1 1.6 %fusion.1 = f32[2,288,512]{2,1,0:T(8,128)S(1)} fusion(bf16[2,432,512]{2,1,0:T(8,128)(2,1)} %reshape.43, bf16[1,288,432]{2,1,0:T(8,128)(2,1)S(1)} %get-tuple-element.28, bf16[1,288,432]{2,1,0:T(8,128)(2,1)S(1)} %bitcast.41), kind=kOutput, calls=%fused_computation.3 | convolution fusion | flops 255052800 | bytes 2562048 | tf_op jit(solution)/shard_map/dot_general | solution.py:105
  100.7 0.4 reshape.44
  101.1 0.1 copy.13
  101.2 25.5 %all_to_all.20 = f32[16,2,72,128]{3,2,1,0:T(8,128)S(1)} all-to-all(f32[16,2,72,128]{3,2,1,0:T(8,128)S(1)} %bitcast.37), channel_id=1, replica_groups=mesh['za'=6,'zb'=2,'ya'=2,'yb'=2,'core'=2,'yhi'=2,'x'=4] {'zb','yb','x'}, dimensions={0} | all-to-all | bytes 2359296 | tf_op jit(solution)/shard_map/all_to_all | solution.py:110
  126.7 0.0 copy-start.4
  126.7 0.1 reduce_sum.9
  126.8 0.6 copy-done.4
  127.4 0.7 add_convert_fusion
  (3 shorter events, 0.0 us)
Async XLA Ops:
  0.0 31.1 %copy-start = (bf16[2,1024,128]{2,1,0:T(8,128)(2,1)S(1)}, bf16[2,1024,128]{2,1,0:T(8,128)(2,1)}, u32[]{:S(2)}) copy-start(bf16[2,1024,128]{2,1,0:T(8,128)(2,1)} %param.9) | copy-start | bytes 1572868
  1.6 20.3 %all-to-all-start.1 = ((bf16[8,2,72,128]{3,2,1,0:T(8,128)(2,1)}), bf16[8,2,72,128]{3,2,1,0:T(8,128)(2,1)S(1)}, u32[]{:S(2)}, u32[]{:S(2)}) async-start(bf16[8,2,72,128]{3,2,1,0:T(8,128)(2,1)} %broadcast_in_dim.4), calls=%async_computation.1 | async-start | bytes 589824 | tf_op jit(solution)/shard_map/all_to_all | solution.py:32
  14.7 15.8 %copy-start.2 = (s32[2]{0:T(128)S(1)}, s32[2]{0:T(128)}, u32[]{:S(2)}) copy-start(s32[2]{0:T(128)} %param.11) | copy-start | bytes 28
  14.7 16.4 %copy-start.1 = (bf16[2,72,128]{2,1,0:T(8,128)(2,1)S(1)}, bf16[2,72,128]{2,1,0:T(8,128)(2,1)}, u32[]{:S(2)}) copy-start(bf16[2,72,128]{2,1,0:T(8,128)(2,1)} %param.8) | copy-start | bytes 110596
  14.7 16.4 %copy-start.3 = (f32[2]{0:T(128)S(1)}, f32[2]{0:T(128)}, u32[]{:S(2)}) copy-start(f32[2]{0:T(128)} %param.12) | copy-start | bytes 28
  21.9 25.6 %all-to-all-start = ((bf16[16,72,432]{2,1,0:T(8,128)(2,1)}), bf16[16,72,432]{2,1,0:T(8,128)(2,1)S(1)}, u32[]{:S(2)}, u32[]{:S(2)}) async-start(bf16[16,72,432]{2,1,0:T(8,128)(2,1)} %shard_map.64), calls=%async_computation | async-start | bytes 2359296 | tf_op jit(solution)/shard_map/all_to_all | solution.py:79
  31.4 14.6 %collective-permute-start.2 = (bf16[2,72,128]{2,1,0:T(8,128)(2,1)S(1)}, bf16[2,72,128]{2,1,0:T(8,128)(2,1)S(1)}, u32[]{:S(2)}, u32[]{:S(2)}) collective-permute-start(bf16[2,72,128]{2,1,0:T(8,128)(2,1)S(1)} %fusion), channel_id=1, source_target_pairs={{0,32},{1,40},{2,0},{3,8},{4,36},{5,44},{6,4},{7,12},{8,33},{9,41}... | collective-permute-start | bytes 110600 | tf_op jit(solution)/shard_map/ppermute | solution.py:75
  35.9 10.1 %collective-permute-start.1 = (bf16[2,72,128]{2,1,0:T(8,128)(2,1)S(1)}, bf16[2,72,128]{2,1,0:T(8,128)(2,1)S(1)}, u32[]{:S(2)}, u32[]{:S(2)}) collective-permute-start(bf16[2,72,128]{2,1,0:T(8,128)(2,1)S(1)} %fusion), channel_id=1, source_target_pairs={{0,0},{1,8},{2,32},{3,40},{4,4},{5,12},{6,36},{7,44},{8,1},{9,9},{... | collective-permute-start | bytes 110600 | tf_op jit(solution)/shard_map/ppermute | solution.py:74
  48.4 38.9 %all-to-all-start.2 = ((bf16[6,2,2,72,128]{4,3,2,1,0:T(8,128)(2,1)}), bf16[6,2,2,72,128]{4,3,2,1,0:T(8,128)(2,1)S(1)}, u32[]{:S(2)}, u32[]{:S(2)}) async-start(bf16[6,2,2,72,128]{4,3,2,1,0:T(8,128)(2,1)} %broadcast_in_dim.5), calls=%async_computation.2 | async-start | bytes 884736 | tf_op jit(solution)/shard_map/all_to_all | solution.py:32
  62.3 25.0 %collective-permute-start.3 = (bf16[288,432]{1,0:T(8,128)(2,1)S(1)}, bf16[288,432]{1,0:T(8,128)(2,1)S(1)}, u32[]{:S(2)}, u32[]{:S(2)}) collective-permute-start(bf16[288,432]{1,0:T(8,128)(2,1)S(1)} %bitcast.42), channel_id=1, source_target_pairs={{0,4},{4,0},{1,5},{5,1},{2,6},{6,2},{3,7},{7,3},{8,12},{12,8},{9,1... | collective-permute-start | bytes 746504 | tf_op jit(solution)/shard_map/ppermute | solution.py:91
  66.4 20.9 %collective-permute-start = (bf16[288,432]{1,0:T(8,128)(2,1)S(1)}, bf16[288,432]{1,0:T(8,128)(2,1)}, u32[]{:S(2)}, u32[]{:S(2)}) collective-permute-start(bf16[288,432]{1,0:T(8,128)(2,1)S(1)} %param.1), channel_id=1, source_target_pairs={{0,4},{4,0},{1,5},{5,1},{2,6},{6,2},{3,7},{7,3},{8,12},{12,8},{9,1... | collective-permute-start | bytes 746504 | tf_op jit(solution)/shard_map/cond/branch_1_fun/ppermute | solution.py:92
  87.3 9.4 %collective-permute-start.4 = (bf16[6,2,2,72,128]{4,3,2,1,0:T(8,128)(2,1)S(1)}, bf16[6,2,2,72,128]{4,3,2,1,0:T(8,128)(2,1)S(1)}, u32[]{:S(2)}, u32[]{:S(2)}) collective-permute-start(bf16[6,2,2,72,128]{4,3,2,1,0:T(8,128)(2,1)S(1)} %all-to-all-done.2), channel_id=1, source_target_pairs={{0,8},{8,0},{1,9},{9,1},{2,10},{10,2},{3,11},{11,3},{4,12},{12,4},... | collective-permute-start | bytes 1327112 | tf_op jit(solution)/shard_map/ppermute | solution.py:102
  126.7 0.7 copy-start.4
